TPU v7x, 256 devices: a whole 4x4x8 slice. The times are simulated.
256 devices in a mesh: row: 32 (over x_hi, z, core), col: 8 (over y, x_lo).
Axes of the slice: x: 4 (x_hi: 2, x_lo: 2; x = x_hi * 2 + x_lo), y: 4, z: 8, core: 2. Of those that a mesh axis runs over, the one named last changes fastest.
Arguments:
- pair: bfloat16 [1024, 1024, 128], P('row', 'col'), may hold values from -6 to 6
- ln_in_gain: float32 [128], replicated, may hold values from 0.1 to 1.9
- proj_left: bfloat16 [128, 256], replicated, may hold values from -0.5 to 0.5
- proj_right: bfloat16 [128, 256], replicated, may hold values from -0.5 to 0.5
- gate_weight: bfloat16 [128, 128], replicated, may hold values from -0.5 to 0.5
- ln_out_gain: float32 [128], replicated, may hold values from 0.1 to 1.9
- out_weight: bfloat16 [128, 128], replicated, may hold values from -0.5 to 0.5
Outputs:
- update: bfloat16 [1024, 1024, 128], P('row', 'col')
All inputs are finite; a program needn't handle non-finite values.
Results may differ from a plain program's by a relative error of at most 0.0083.
Values may be sent and summed in bfloat16 or wider, within the bound.
No kernel may reach another device: no remote copies, remote signals or barrier semaphores. Data moves between devices by JAX's collectives and lax.ppermute only.
A program may use at most 64 MiB of HBM per device.

v0:
```python
import jax
import jax.numpy as jnp
from jax import lax
from jax.sharding import PartitionSpec as P


def layer_norm(values, scale_gain, dimension):
    average = jnp.mean(values, axis=dimension, keepdims=True)
    centered = values - average
    spread = jnp.mean(centered * centered, axis=dimension, keepdims=True)
    return centered * lax.rsqrt(spread + 1e-05) * scale_gain


def gated_pair(normed, weights, width):
    both = jnp.einsum("rcd,de->erc", normed, weights, preferred_element_type=jnp.float32)
    return (jax.nn.sigmoid(both[:width]) * both[width:]).astype(jnp.bfloat16)


def shards(pair, ln_in_gain, proj_left, proj_right, gate_weight, ln_out_gain, out_weight):
    width = out_weight.shape[0]
    normed = layer_norm(pair.astype(jnp.float32), ln_in_gain, -1).astype(jnp.bfloat16)
    left_side = gated_pair(normed, proj_left, width)
    right_side = gated_pair(normed, proj_right, width)
    gating = jax.nn.sigmoid(
        jnp.einsum("rcd,de->rce", normed, gate_weight, preferred_element_type=jnp.float32)
    )
    left_panel, right_panel = (
        lax.all_to_all(
            lax.all_to_all(left_side, "row", split_axis=0, concat_axis=1, tiled=True),
            "col",
            split_axis=1,
            concat_axis=2,
            tiled=True,
        ),
        lax.all_to_all(
            lax.all_to_all(right_side, "row", split_axis=0, concat_axis=1, tiled=True),
            "col",
            split_axis=1,
            concat_axis=2,
            tiled=True,
        ),
    )
    product = jnp.einsum(
        "hik,hjk->hij",
        left_panel,
        lax.all_gather(right_panel, "col", axis=1, tiled=True),
        preferred_element_type=jnp.float32,
    )
    product_half = product.astype(jnp.bfloat16)
    by_owner = lax.all_to_all(
        lax.all_to_all(product_half, "col", split_axis=2, concat_axis=1, tiled=True),
        "row",
        split_axis=1,
        concat_axis=0,
        tiled=True,
    )
    product_norm = layer_norm(
        by_owner.astype(jnp.float32), ln_out_gain.reshape(-1, 1, 1), 0
    ).astype(jnp.bfloat16)
    projected = jnp.einsum(
        "hrc,hd->rcd", product_norm, out_weight, preferred_element_type=jnp.float32
    )
    return (gating * projected).astype(jnp.bfloat16)


def solution(mesh):
    in_specs = (P("row", "col", None), P(), P(), P(), P(), P(), P())
    out_specs = P("row", "col", None)
    return jax.shard_map(shards, mesh=mesh, in_specs=in_specs, out_specs=out_specs, check_vma=False)
```

profile of v0, /device:TPU:1, one launch (start us, length us, event | category | flops | bytes accessed | tf_op | source)
XLA Modules:
  0.0 345.9 jit_solution(13630515080666360546)
XLA Ops:
  6.5 0.0 copy-start
  6.5 0.0 all-gather.2.cloned.1.call-start
  6.5 1.7 convert_reduce_fusion
  8.2 2.3 fusion.2
  10.6 0.0 copy-done
  10.6 0.0 copy-done.1
  10.6 0.0 copy-done.5
  10.6 1.5 convolution_bitcast_fusion
  12.1 0.6 fusion.5
  12.7 1.0 copy.37
  13.7 40.1 %all_to_all.99 = bf16[128,32,128]{2,1,0:T(8,128)(2,1)S(1)} all-to-all(bf16[128,32,128]{2,1,0:T(8,128)(2,1)S(1)} %copy.37), channel_id=1, replica_groups=mesh['row'=32,'col'=8] {'row'}, dimensions={0} | all-to-all | bytes 2097152 | tf_op jit(solution)/shard_map/all_to_all | solution.py:36
  53.8 0.1 copy.38
  53.9 0.8 copy.39
  54.7 17.0 %all_to_all.100 = bf16[4,1024,128]{2,0,1:T(4,128)(2,1)S(1)} all-to-all(bf16[4,1024,128]{2,0,1:T(4,128)(2,1)S(1)} %copy.39), channel_id=1, replica_groups=mesh['row'=32,'col'=8] {'col'}, dimensions={1} | all-to-all | bytes 2097152 | tf_op jit(solution)/shard_map/all_to_all | solution.py:35
  71.7 0.1 copy.40
  71.9 0.0 copy-start.3
  71.9 1.3 copy.60
  73.2 0.0 all-gather.2.cloned.1.call-update
  73.2 0.0 copy-done.3
  73.2 1.5 convolution_bitcast_fusion.1
  74.7 0.6 fusion.9
  75.3 1.0 copy.32
  76.3 37.6 %all_to_all.101 = bf16[128,32,128]{2,1,0:T(8,128)(2,1)S(1)} all-to-all(bf16[128,32,128]{2,1,0:T(8,128)(2,1)S(1)} %copy.32), channel_id=1, replica_groups=mesh['row'=32,'col'=8] {'row'}, dimensions={0} | all-to-all | bytes 2097152 | tf_op jit(solution)/shard_map/all_to_all | solution.py:29
  113.8 0.1 copy.33
  113.9 0.8 copy.34
  114.7 29.0 %all_to_all.102 = bf16[4,1024,128]{2,0,1:T(4,128)(2,1)S(1)} all-to-all(bf16[4,1024,128]{2,0,1:T(4,128)(2,1)S(1)} %copy.34), channel_id=1, replica_groups=mesh['row'=32,'col'=8] {'col'}, dimensions={1} | all-to-all | bytes 2097152 | tf_op jit(solution)/shard_map/all_to_all | solution.py:28
  143.8 0.1 copy.35
  143.9 121.9 %all-gather.2.cloned.1.call-done = bf16[4,1024,1024]{2,1,0:T(8,128)(2,1)} async-done(((bf16[4,128,1024]{2,1,0:T(8,128)(2,1)}), bf16[4,1024,1024]{2,1,0:T(8,128)(2,1)}) %all-gather.2.cloned.1.call-update) | async-done | bytes 8388624 | tf_op jit(solution)/shard_map/all_gather | solution.py:46
  265.8 6.3 %convolution_convert_fusion = bf16[4,128,1024]{2,1,0:T(8,128)(2,1)S(1)} fusion(bf16[4,1024,1024]{2,1,0:T(8,128)(2,1)} %all-gather.2.cloned.1.call-done, bf16[4,8,16,8,128]{4,3,2,1,0:T(8,128)(2,1)S(1)} %bitcast.62), kind=kOutput, calls=%fused_computation.28 | convolution fusion | flops 1074266112 | bytes 10485760 | tf_op jit(solution)/shard_map/hik,hjk->hij/dot_general | solution.py:43
  272.1 0.8 copy.42
  272.9 19.4 %all_to_all.103 = bf16[4,128,1024]{1,0,2:T(4,128)(2,1)S(1)} all-to-all(bf16[4,128,1024]{1,0,2:T(4,128)(2,1)S(1)} %copy.42), channel_id=1, replica_groups=mesh['row'=32,'col'=8] {'col'}, dimensions={2} | all-to-all | bytes 2097152 | tf_op jit(solution)/shard_map/all_to_all | solution.py:51
  292.2 0.1 copy.43
  292.4 0.7 copy.44
  293.0 0.0 copy-start.4
  293.1 1.8 copy.45
  294.8 11.4 %all-to-all-start.5 = ((bf16[4,1024,128]{2,0,1:T(4,128)(2,1)}), bf16[4,1024,128]{2,0,1:T(4,128)(2,1)S(1)}, u32[]{:S(2)}, u32[]{:S(2)}) async-start(bf16[4,1024,128]{2,0,1:T(4,128)(2,1)} %copy.45), calls=%async_computation.5 | async-start | bytes 2097152 | tf_op jit(solution)/shard_map/all_to_all | solution.py:50
  306.3 2.5 fusion.22
  308.8 25.2 %all-to-all-done.5 = bf16[4,1024,128]{2,0,1:T(4,128)(2,1)S(1)} async-done(((bf16[4,1024,128]{2,0,1:T(4,128)(2,1)}), bf16[4,1024,128]{2,0,1:T(4,128)(2,1)S(1)}, u32[]{:S(2)}, u32[]{:S(2)}) %all-to-all-start.5) | async-done | bytes 1048608 | tf_op jit(solution)/shard_map/all_to_all | solution.py:50
  334.0 0.3 fusion.28
  334.3 0.2 fusion.16
  334.5 0.3 multiply_reduce_fusion
  334.9 0.0 copy-start.6
  334.9 0.2 copy.47
  335.1 0.4 copy-done.6
  335.5 0.3 fusion.15
  335.8 1.3 copy-done.2
  337.1 0.0 copy-done.7
  337.1 2.0 multiply_convert_fusion
  (9 shorter events, 0.0 us)
Async XLA Ops:
  6.5 4.1 %copy-start = (bf16[128,256]{1,0:T(8,128)(2,1)S(1)}, bf16[128,256]{1,0:T(8,128)(2,1)}, u32[]{:S(2)}) copy-start(bf16[128,256]{1,0:T(8,128)(2,1)} %param.10) | copy-start | bytes 196612
  6.5 4.1 %copy-start.1 = (bf16[32,128,128]{2,1,0:T(8,128)(2,1)S(1)}, bf16[32,128,128]{2,1,0:T(8,128)(2,1)}, u32[]{:S(2)}) copy-start(bf16[32,128,128]{2,1,0:T(8,128)(2,1)} %param.7) | copy-start | bytes 3145732
  6.5 4.1 %copy-start.5 = (f32[128]{0:T(128)S(1)}, f32[128]{0:T(128)}, u32[]{:S(2)}) copy-start(f32[128]{0:T(128)} %param.8) | copy-start | bytes 1540
  6.5 259.3 %all-gather.2.cloned.1.call-start = ((), (), s32[]{:S(2)}) async-start(), calls=%async_computation.6 | async-start | bytes 9437184 | tf_op jit(solution)/shard_map/all_gather | solution.py:46
  71.9 1.3 copy-start.3
  293.0 13.2 %copy-start.4 = (bf16[128,128]{1,0:T(8,128)(2,1)S(1)}, bf16[128,128]{1,0:T(8,128)(2,1)}, u32[]{:S(2)}) copy-start(bf16[128,128]{1,0:T(8,128)(2,1)} %param.11) | copy-start | bytes 98308
  294.8 39.2 %all-to-all-start.5 = ((bf16[4,1024,128]{2,0,1:T(4,128)(2,1)}), bf16[4,1024,128]{2,0,1:T(4,128)(2,1)S(1)}, u32[]{:S(2)}, u32[]{:S(2)}) async-start(bf16[4,1024,128]{2,0,1:T(4,128)(2,1)} %copy.45), calls=%async_computation.5 | async-start | bytes 2097152 | tf_op jit(solution)/shard_map/all_to_all | solution.py:50
  334.9 0.7 copy-start.6
  335.5 1.6 copy-start.2
  335.5 1.6 copy-start.7
Sparse Core Ops, SparseCore 0:
  73.3 192.4 all-gather.1
where the time goes:
time: 348 us; the launch traced here: 346 us
  waiting for transfers between devices  147 us (42%)
  blocking collectives  143 us (41%)
  matrix products  13.8 us (4%)
  between operations  13.6 us (4%)
  starting transfers between devices  11.4 us (3%)
  local copies, waits for them, and re-layouts  10.5 us (3%)
  other arithmetic  6.25 us (2%)
    all_gather x1, waiting for transfers between devices, shards(): lax.all_gather(right_panel, 'col', axis=1, tiled=True)  122 us
    all_to_all x1, blocking collectives, shards(): lax.all_to_all(right_side, 'row', split_axis=0, concat_axis=1, tiled=True)  40.1 us
    all_to_all x1, blocking collectives, shards(): lax.all_to_all(left_side, 'row', split_axis=0, concat_axis=1, tiled=True)  37.6 us
    all_to_all x1, blocking collectives, shards(): lax.all_to_all(lax.all_to_all(left_side, 'row', split_axis=0, concat_axis...  29 us
    all_to_all x1, waiting for transfers between devices, shards(): lax.all_to_all(lax.all_to_all(product_half, 'col', split_axis=2, concat_a...  25.2 us
    all_to_all x1, blocking collectives, shards(): lax.all_to_all(product_half, 'col', split_axis=2, concat_axis=1, tiled=True)  19.4 us
    all_to_all x1, blocking collectives, shards(): lax.all_to_all(lax.all_to_all(right_side, 'row', split_axis=0, concat_axi...  17 us
    all_to_all x1, starting transfers between devices, shards(): lax.all_to_all(lax.all_to_all(product_half, 'col', split_axis=2, concat_a...  11.4 us
  transfers between devices with their start and end apart: 2, of which 2 were waited for; matrix products, arithmetic and copies ran while one was open for 2% of the time, Pallas kernels for 0%

commit v1 on v0

v1 whole, which is shorter than its diff:
```python
import jax
import jax.numpy as jnp
from jax import lax
from jax.sharding import PartitionSpec as P


def layer_norm(values, scale_gain, dimension):
    average = jnp.mean(values, axis=dimension, keepdims=True)
    centered = values - average
    spread = jnp.mean(centered * centered, axis=dimension, keepdims=True)
    return centered * lax.rsqrt(spread + 1e-05) * scale_gain


def gated_pair(normed, weights, width):
    both = jnp.einsum("rcd,de->erc", normed, weights, preferred_element_type=jnp.float32)
    return (jax.nn.sigmoid(both[:width]) * both[width:]).astype(jnp.bfloat16)


def shards(rows, cols, pair, ln_in_gain, proj_left, proj_right, gate_weight, ln_out_gain, out_weight):
    width = out_weight.shape[0]
    here_i, here_k = pair.shape[0], pair.shape[1]
    half = here_i // 2
    chips = rows // 2
    normed = layer_norm(pair.astype(jnp.float32), ln_in_gain, -1).astype(jnp.bfloat16)
    left_side = gated_pair(normed, proj_left, width)
    right_side = gated_pair(normed, proj_right, width)
    gating = jax.nn.sigmoid(
        jnp.einsum("rcd,de->rce", normed, gate_weight, preferred_element_type=jnp.float32)
    )

    def by_device(side):
        side = side.reshape(chips, cols, 2, half, here_k)
        return jnp.swapaxes(side, 1, 2).reshape(rows * cols, half, here_k)

    sent = jnp.stack([by_device(left_side), by_device(right_side)], axis=1)
    got = lax.all_to_all(sent, ("row", "col"), split_axis=0, concat_axis=0, tiled=True)

    def panel(one):
        one = one.reshape(rows, cols, half, here_k)
        return jnp.swapaxes(one, 1, 2).reshape(rows, half, cols * here_k)

    left_panel, right_own = panel(got[:, 0]), panel(got[:, 1])
    right_other = lax.ppermute(right_own, "row", [(r, r ^ 1) for r in range(rows)])
    first_core = lax.axis_index("row") % 2 == 0
    right_panel = jnp.stack(
        [
            jnp.where(first_core, right_own, right_other),
            jnp.where(first_core, right_other, right_own),
        ],
        axis=1,
    ).reshape(rows * here_i, cols * here_k)
    product = jnp.einsum(
        "rik,jk->rij", left_panel, right_panel, preferred_element_type=jnp.float32
    ).astype(jnp.bfloat16)
    product = product.reshape(rows, half, cols, here_k)
    product = jnp.swapaxes(product, 1, 2).reshape(rows * cols, half, here_k)
    back = lax.all_to_all(product, ("row", "col"), split_axis=0, concat_axis=0, tiled=True)
    by_owner = jnp.swapaxes(back.reshape(chips, 2, cols, half, here_k), 1, 2)
    by_owner = by_owner.reshape(width, here_i, here_k)
    product_norm = layer_norm(
        by_owner.astype(jnp.float32), ln_out_gain.reshape(-1, 1, 1), 0
    ).astype(jnp.bfloat16)
    projected = jnp.einsum(
        "hrc,hd->rcd", product_norm, out_weight, preferred_element_type=jnp.float32
    )
    return (gating * projected).astype(jnp.bfloat16)


def solution(mesh):
    rows, cols = mesh.shape["row"], mesh.shape["col"]
    in_specs = (P("row", "col", None), P(), P(), P(), P(), P(), P())
    out_specs = P("row", "col", None)

    def step(*arrays):
        return shards(rows, cols, *arrays)

    return jax.shard_map(step, mesh=mesh, in_specs=in_specs, out_specs=out_specs, check_vma=False)
```

time: 348 us -> 133 us (0.38)
  waiting for transfers between devices: 147 us -> 30.7 us
  blocking collectives: 143 us -> 68.6 us
  between operations: 13.6 us -> 0.26 us
  matrix products: 13.8 us -> 8.68 us
  starting transfers between devices: 11.4 us -> 6.65 us
    all_gather x1 -> x0, waiting for transfers between devices: 122 us -> none  [shards(): lax.all_gather(right_panel, 'col', axis=1, tiled=True)]
    all_to_all x5 -> x1, blocking collectives: 143 us -> 68.6 us  [shards(): lax.all_to_all(sent, ('row', 'col'), split_axis=0, concat_axis=0, tiled=T...]
    all_to_all x10 -> x0, local copies, waits for them, and re-layouts: 5.89 us -> none  [the longest x3 2.58 us: shards(): lax.all_to_all(product_half, 'col', split_axis=2, concat_axis=1, tiled=True)]
    dot_general x1, matrix products: 6.28 us -> 1.29 us  [shards(): jnp.einsum('rik,jk->rij', left_panel, right_panel, preferred_element_type...]
    all_to_all x1, starting transfers between devices: 11.4 us -> 6.65 us  [shards(): lax.all_to_all(product, ('row', 'col'), split_axis=0, concat_axis=0, tile...]
where the time goes in v1:
time: 133 us
  blocking collectives  68.6 us (52%)
  waiting for transfers between devices  30.7 us (23%)
  local copies, waits for them, and re-layouts  11.2 us (8%)
  matrix products  8.68 us (7%)
  other arithmetic  6.7 us (5%)
  starting transfers between devices  6.65 us (5%)
    all_to_all x1, blocking collectives, shards(): lax.all_to_all(sent, ('row', 'col'), split_axis=0, concat_axis=0, tiled=T...  68.6 us
    all_to_all x1, waiting for transfers between devices, shards(): lax.all_to_all(product, ('row', 'col'), split_axis=0, concat_axis=0, tile...  27.8 us
    all_to_all x1, starting transfers between devices, shards(): lax.all_to_all(product, ('row', 'col'), split_axis=0, concat_axis=0, tile...  6.65 us
    unnamed x20, local copies, waits for them, and re-layouts  3.16 us
    dot_general x2, matrix products, gated_pair(): jnp.einsum('rcd,de->erc', normed, weights, preferred_element_type=jnp.flo...  3.02 us
    ppermute x1, waiting for transfers between devices, shards(): lax.ppermute(right_own, 'row', [(r, r ^ 1) for r in range(rows)])  2.87 us
  transfers between devices with their start and end apart: 2, of which 2 were waited for; matrix products, arithmetic and copies ran while one was open for 2% of the time, Pallas kernels for 0%

profile of v1, /device:TPU:1, one launch (start us, length us, event | category | flops | bytes accessed | tf_op | source)
XLA Modules:
  0.0 132.8 jit_solution(7220325642743776825)
XLA Ops:
  0.0 0.0 copy-start
  0.0 1.7 %convert_reduce_fusion = f32[32,128]{1,0:T(8,128)S(1)} fusion(bf16[32,128,128]{2,1,0:T(8,128)(2,1)} %param.7), kind=kLoop, calls=%fused_computation.1 | loop fusion | flops 1044480 | bytes 1064960 | tf_op jit(solution)/shard_map/reduce_sum | solution.py:8
  1.7 2.3 %fusion.2 = f32[32,128]{1,0:T(8,128)S(1)} fusion(bf16[32,128,128]{2,1,0:T(8,128)(2,1)} %param.7, f32[32,128]{1,0:T(8,128)S(1)} %broadcast_multiply_fusion.1), kind=kLoop, calls=%fused_computation.6 | loop fusion | flops 2093056 | bytes 1081344 | tf_op jit(solution)/shard_map/reduce_sum | solution.py:10
  4.0 0.0 copy-done
  4.1 0.0 copy-done.1
  4.1 0.0 copy-done.7
  4.1 1.5 %convolution_bitcast_fusion = f32[256,32,128]{0,2,1:T(8,128)S(1)} fusion(bf16[32,128,128]{2,1,0:T(8,128)(2,1)S(1)} %copy-done.1, f32[128]{0:T(128)S(1)} %copy-done.7, f32[32,128]{1,0:T(8,128)S(1)} %add_rsqrt_fusion.1, f32[32,128]{1,0:T(8,128)S(1)} %broadcast_multiply_fusion.1, bf16[128,256]{1,0:T(8,128)(2,1)S(1)} %copy-done), kind=kOutput, calls=%fused_computation.4 | convolution fusion | flops 271056896 | bytes 5341696 | tf_op jit(solution)/shard_map/rcd,de->erc/dot_general | solution.py:15
  5.6 0.6 fusion.5
  6.2 0.0 copy-start.5
  6.2 1.0 copy.30
  7.2 1.2 copy.31
  8.4 0.0 copy-done.5
  8.4 1.5 %convolution_bitcast_fusion.1 = f32[256,32,128]{0,2,1:T(8,128)S(1)} fusion(bf16[32,128,128]{2,1,0:T(8,128)(2,1)S(1)} %copy-done.1, f32[128]{0:T(128)S(1)} %copy-done.7, f32[32,128]{1,0:T(8,128)S(1)} %add_rsqrt_fusion.1, f32[32,128]{1,0:T(8,128)S(1)} %broadcast_multiply_fusion.1, bf16[128,256]{1,0:T(8,128)(2,1)S(1)} %copy-done.5), kind=kOutput, calls=%fused_computation.5 | convolution fusion | flops 271056896 | bytes 5341696 | tf_op jit(solution)/shard_map/rcd,de->erc/dot_general | solution.py:15
  9.9 0.6 fusion.9
  10.5 1.0 copy.28
  11.4 0.0 copy-start.2
  11.5 0.2 copy.29
  11.7 1.0 copy-done.2
  12.7 0.2 pad_maximum_fusion
  12.9 0.4 copy.32
  13.2 68.6 %all_to_all.10 = bf16[256,2,16,128]{3,2,1,0:T(8,128)(2,1)S(1)} all-to-all(bf16[256,2,16,128]{3,2,1,0:T(8,128)(2,1)S(1)} %copy.32), channel_id=1, replica_groups=mesh['row'=32,'col'=8] {'row','col'}, dimensions={0} | all-to-all | bytes 4194304 | tf_op jit(solution)/shard_map/all_to_all | solution.py:36
  81.8 1.3 %fusion.26 = (bf16[256,1,16,128]{3,2,1,0:T(8,128)(2,1)}, bf16[256,1,16,128]{3,2,1,0:T(8,128)(2,1)S(1)}) fusion(bf16[256,2,16,128]{3,2,1,0:T(8,128)(2,1)S(1)} %all_to_all.10), kind=kLoop, calls=%fused_computation.46 | loop fusion | bytes 4194304 | tf_op jit(solution)/shard_map/slice | solution.py:42
  83.2 1.2 copy.58
  84.4 0.0 collective-permute-start
  84.4 2.9 %collective-permute-done = bf16[32,16,1024]{2,1,0:T(8,128)(2,1)S(1)} collective-permute-done((bf16[32,16,1024]{2,1,0:T(8,128)(2,1)}, bf16[32,16,1024]{2,1,0:T(8,128)(2,1)S(1)}, u32[]{:S(2)}, u32[]{:S(2)}) %collective-permute-start) | collective-permute-done | bytes 1048608 | tf_op jit(solution)/shard_map/ppermute | solution.py:43
  87.2 0.1 select_bitcast_fusion.1
  87.4 0.2 pad_maximum_fusion.1
  87.6 0.0 copy-start.4
  87.6 0.3 copy.37
  87.9 0.9 copy-done.4
  88.8 1.3 fusion.13
  90.1 0.0 copy-start.6
  90.1 1.2 copy.59
  91.3 6.7 %all-to-all-start.1 = ((bf16[256,16,128]{2,1,0:T(8,128)(2,1)}), bf16[256,16,128]{2,1,0:T(8,128)(2,1)S(1)}, u32[]{:S(2)}, u32[]{:S(2)}) async-start(bf16[256,16,128]{2,1,0:T(8,128)(2,1)} %bitcast.20), calls=%async_computation.1 | async-start | bytes 2097152 | tf_op jit(solution)/shard_map/all_to_all | solution.py:57
  98.0 0.0 copy-done.6
  98.0 2.5 %fusion.20 = f32[32,128,128]{2,1,0:T(8,128)} fusion(bf16[32,128,128]{2,1,0:T(8,128)(2,1)S(1)} %copy-done.1, f32[128]{0:T(128)S(1)} %copy-done.7, f32[32,128]{1,0:T(8,128)S(1)} %add_rsqrt_fusion.1, f32[32,128]{1,0:T(8,128)S(1)} %broadcast_multiply_fusion.1, bf16[128,128]{1,0:T(8,128)(2,1)S(1)} %copy-done.6), kind=kOutput, calls=%fused_computation.37 | convolution fusion | flops 136839168 | bytes 3211776 | tf_op jit(solution)/shard_map/rcd,de->rce/dot_general | solution.py:28
  100.5 27.8 %all-to-all-done.1 = bf16[256,16,128]{2,1,0:T(8,128)(2,1)S(1)} async-done(((bf16[256,16,128]{2,1,0:T(8,128)(2,1)}), bf16[256,16,128]{2,1,0:T(8,128)(2,1)S(1)}, u32[]{:S(2)}, u32[]{:S(2)}) %all-to-all-start.1) | async-done | bytes 1048608 | tf_op jit(solution)/shard_map/all_to_all | solution.py:57
  128.3 0.2 fusion.14
  128.5 0.3 multiply_reduce_fusion
  128.8 0.3 convert_bitcast_fusion
  129.0 0.0 copy-start.8
  129.1 0.3 copy.39
  129.3 0.0 copy-start.3
  129.3 0.0 copy-start.9
  129.3 0.4 copy-done.8
  129.7 0.3 multiply_convert_fusion.1
  130.0 0.9 copy-done.3
  130.9 1.9 %multiply_convert_fusion = bf16[32,128,128]{2,1,0:T(8,128)(2,1)} fusion(f32[32,128,128]{2,1,0:T(8,128)S(1)} %copy-done.3, bf16[128,32,128]{2,1,0:T(8,128)(2,1)S(1)} %multiply_convert_fusion.1, bf16[128,128]{1,0:T(8,128)(2,1)S(1)} %copy-done.9), kind=kOutput, calls=%fused_computation.24 | convolution fusion | flops 136839168 | bytes 4227072 | tf_op jit(solution)/shard_map/hrc,hd->rcd/dot_general | solution.py:63
  (7 shorter events, 0.0 us)
Async XLA Ops:
  0.0 4.0 %copy-start = (bf16[128,256]{1,0:T(8,128)(2,1)S(1)}, bf16[128,256]{1,0:T(8,128)(2,1)}, u32[]{:S(2)}) copy-start(bf16[128,256]{1,0:T(8,128)(2,1)} %param.10) | copy-start | bytes 196612
  0.0 4.1 %copy-start.1 = (bf16[32,128,128]{2,1,0:T(8,128)(2,1)S(1)}, bf16[32,128,128]{2,1,0:T(8,128)(2,1)}, u32[]{:S(2)}) copy-start(bf16[32,128,128]{2,1,0:T(8,128)(2,1)} %param.7) | copy-start | bytes 3145732
  0.0 4.1 %copy-start.7 = (f32[128]{0:T(128)S(1)}, f32[128]{0:T(128)}, u32[]{:S(2)}) copy-start(f32[128]{0:T(128)} %param.8) | copy-start | bytes 1540
  6.2 2.2 %copy-start.5 = (bf16[128,256]{1,0:T(8,128)(2,1)S(1)}, bf16[128,256]{1,0:T(8,128)(2,1)}, u32[]{:S(2)}) copy-start(bf16[128,256]{1,0:T(8,128)(2,1)} %param.9) | copy-start | bytes 196612
  11.4 1.2 copy-start.2
  84.4 2.9 %collective-permute-start = (bf16[32,16,1024]{2,1,0:T(8,128)(2,1)}, bf16[32,16,1024]{2,1,0:T(8,128)(2,1)S(1)}, u32[]{:S(2)}, u32[]{:S(2)}) collective-permute-start(bf16[32,16,1024]{2,1,0:T(8,128)(2,1)} %bitcast.72), channel_id=1, source_target_pairs={{0,8},{8,0},{16,24},{24,16},{32,40},{40,32},{48,56},{56,48},{64,72... | collective-permute-start | bytes 3145736 | tf_op jit(solution)/shard_map/ppermute | solution.py:43
  87.6 1.2 copy-start.4
  90.1 7.8 %copy-start.6 = (bf16[128,128]{1,0:T(8,128)(2,1)S(1)}, bf16[128,128]{1,0:T(8,128)(2,1)}, u32[]{:S(2)}) copy-start(bf16[128,128]{1,0:T(8,128)(2,1)} %param.11) | copy-start | bytes 98308
  91.3 37.0 %all-to-all-start.1 = ((bf16[256,16,128]{2,1,0:T(8,128)(2,1)}), bf16[256,16,128]{2,1,0:T(8,128)(2,1)S(1)}, u32[]{:S(2)}, u32[]{:S(2)}) async-start(bf16[256,16,128]{2,1,0:T(8,128)(2,1)} %bitcast.20), calls=%async_computation.1 | async-start | bytes 2097152 | tf_op jit(solution)/shard_map/all_to_all | solution.py:57
  129.0 0.7 copy-start.8
  129.3 1.6 %copy-start.3 = (f32[32,128,128]{2,1,0:T(8,128)S(1)}, f32[32,128,128]{2,1,0:T(8,128)}, u32[]{:S(2)}) copy-start(f32[32,128,128]{2,1,0:T(8,128)} %fusion.20) | copy-start | bytes 6291460
  129.3 1.6 %copy-start.9 = (bf16[128,128]{1,0:T(8,128)(2,1)S(1)}, bf16[128,128]{1,0:T(8,128)(2,1)}, u32[]{:S(2)}) copy-start(bf16[128,128]{1,0:T(8,128)(2,1)} %param.13) | copy-start | bytes 98308

commit v2 on v1

v2 whole, which is shorter than its diff:
```python
import functools

import jax
import jax.numpy as jnp
from jax import lax
from jax.experimental import pallas as pl
from jax.experimental.pallas import tpu as pltpu
from jax.sharding import PartitionSpec as P

F32, BF16 = jnp.float32, jnp.bfloat16
VMEM_LIMIT = 40 * 1024 * 1024


def sigmoid(values):
    return 0.5 * jnp.tanh(0.5 * values) + 0.5


def normalize(values, gain):
    average = jnp.mean(values, axis=-1, keepdims=True)
    centered = values - average
    spread = jnp.mean(centered * centered, axis=-1, keepdims=True)
    return (centered * lax.rsqrt(spread + 1e-05) * gain).astype(BF16)


def operands_kernel(pair_ref, gain_ref, left_ref, right_ref, sent_ref, turned, sides):
    half, here_k, channels = pair_ref.shape
    width = left_ref.shape[1] // 2
    turned[0] = left_ref[...].astype(F32).T.astype(BF16)
    turned[1] = right_ref[...].astype(F32).T.astype(BF16)
    gain = gain_ref[...]
    for i in range(0, half, 2):
        rows = pair_ref[i : i + 2].reshape(2 * here_k, channels).astype(F32)
        normed = normalize(rows, gain)
        for side in range(2):
            both = lax.dot_general(
                turned[side], normed, (((1,), (1,)), ((), ())), preferred_element_type=F32
            )
            gated = sigmoid(both[:width]) * both[width:]
            sides[side, i] = gated[:, :here_k]
            sides[side, i + 1] = gated[:, here_k:]
    for side in range(2):
        by_channel = jnp.swapaxes(sides[side], 0, 1).astype(BF16)
        chips, _, cols = sent_ref.shape[:3]
        sent_ref[:, 0, :, side] = by_channel.reshape(chips, cols, half, here_k)


def operands(pair, gain, proj_left, proj_right, chips, cols):
    here_i, here_k, channels = pair.shape
    half, width = here_i // 2, proj_left.shape[1] // 2
    whole = lambda array: pl.BlockSpec(array.shape, lambda c: (0,) * array.ndim)
    return pl.pallas_call(
        operands_kernel,
        grid=(2,),
        in_specs=[
            pl.BlockSpec((half, here_k, channels), lambda c: (c, 0, 0)),
            whole(gain),
            whole(proj_left),
            whole(proj_right),
        ],
        out_specs=pl.BlockSpec((chips, 1, cols, 2, half, here_k), lambda c: (0, c, 0, 0, 0, 0)),
        out_shape=jax.ShapeDtypeStruct((chips, 2, cols, 2, half, here_k), BF16),
        scratch_shapes=[
            pltpu.VMEM((2, 2 * width, channels), BF16),
            pltpu.VMEM((2, half, width, here_k), F32),
        ],
        compiler_params=pltpu.CompilerParams(vmem_limit_bytes=VMEM_LIMIT),
        name="operands",
    )(pair, gain, proj_left, proj_right)


def triangle_kernel(core_ref, got_ref, other_ref, product_ref, left, right):
    rows, cols, _, half, here_k = got_ref.shape
    core = core_ref[0]
    for s in range(cols):
        span = pl.ds(s * here_k, here_k)
        left[:, span] = got_ref[:, s, 0].reshape(rows * half, here_k)
        right[:, core, :, span] = got_ref[:, s, 1]
        right[:, 1 - core, :, span] = other_ref[:, s]
    each = rows // cols
    for s in range(0, cols, 2):
        part = right[s * each : (s + 2) * each].reshape(2 * here_k, cols * here_k)
        total = lax.dot_general(
            left[...], part, (((1,), (1,)), ((), ())), preferred_element_type=F32
        ).astype(BF16)
        product_ref[:, s] = total[:, :here_k].reshape(rows, half, here_k)
        product_ref[:, s + 1] = total[:, here_k:].reshape(rows, half, here_k)


def triangle(core, got, other):
    rows, cols, _, half, here_k = got.shape
    vmem = pl.BlockSpec(memory_space=pltpu.VMEM)
    return pl.pallas_call(
        triangle_kernel,
        in_specs=[pl.BlockSpec(memory_space=pltpu.SMEM), vmem, vmem],
        out_specs=vmem,
        out_shape=jax.ShapeDtypeStruct((rows, cols, half, here_k), BF16),
        scratch_shapes=[
            pltpu.VMEM((rows * half, cols * here_k), BF16),
            pltpu.VMEM((rows, 2, half, cols * here_k), BF16),
        ],
        compiler_params=pltpu.CompilerParams(vmem_limit_bytes=VMEM_LIMIT),
        name="triangle",
    )(core, got, other)


def gate_kernel(pair_ref, gain_ref, weight_ref, gate_ref):
    some, here_k, channels = pair_ref.shape
    rows = pair_ref[...].reshape(some * here_k, channels).astype(F32)
    normed = normalize(rows, gain_ref[...])
    gate = sigmoid(jnp.dot(normed, weight_ref[...], preferred_element_type=F32))
    gate_ref[...] = gate.reshape(gate_ref.shape)


def gates(pair, gain, weight):
    here_i, here_k, channels = pair.shape
    some = here_i // 4
    block = pl.BlockSpec((some, here_k, channels), lambda i: (i, 0, 0))
    return pl.pallas_call(
        gate_kernel,
        grid=(4,),
        in_specs=[
            block,
            pl.BlockSpec(gain.shape, lambda i: (0, 0)),
            pl.BlockSpec(weight.shape, lambda i: (0, 0)),
        ],
        out_specs=block,
        out_shape=jax.ShapeDtypeStruct(pair.shape, F32),
        compiler_params=pltpu.CompilerParams(vmem_limit_bytes=VMEM_LIMIT),
        cost_estimate=pl.CostEstimate(
            flops=2 * pair.size * channels, bytes_accessed=6 * pair.size, transcendentals=pair.size
        ),
        name="gates",
    )(pair, gain, weight)


def update_kernel(back_ref, gain_ref, weight_ref, gate_ref, update_ref):
    chips, _, cols, half, here_k = back_ref.shape
    width = chips * cols
    product = back_ref[...].reshape(width, half, here_k).astype(F32)
    average = jnp.mean(product, axis=0, keepdims=True)
    centered = product - average
    spread = jnp.mean(centered * centered, axis=0, keepdims=True)
    normed = centered * lax.rsqrt(spread + 1e-05)
    normed = (jnp.swapaxes(normed, 0, 1) * gain_ref[...]).astype(BF16)
    for i in range(half):
        projected = lax.dot_general(
            normed[i], weight_ref[...], (((0,), (0,)), ((), ())), preferred_element_type=F32
        )
        update_ref[i] = (gate_ref[i] * projected).astype(BF16)


def updates(back, gain, weight, gate):
    chips, _, cols, half, here_k = back.shape
    here_i, _, channels = gate.shape
    block = pl.BlockSpec((half, here_k, channels), lambda c: (c, 0, 0))
    return pl.pallas_call(
        update_kernel,
        grid=(2,),
        in_specs=[
            pl.BlockSpec((chips, 1, cols, half, here_k), lambda c: (0, c, 0, 0, 0)),
            pl.BlockSpec(gain.shape, lambda c: (0, 0)),
            pl.BlockSpec(weight.shape, lambda c: (0, 0)),
            block,
        ],
        out_specs=block,
        out_shape=jax.ShapeDtypeStruct((here_i, here_k, channels), BF16),
        compiler_params=pltpu.CompilerParams(vmem_limit_bytes=VMEM_LIMIT),
        name="updates",
    )(back, gain, weight, gate)


def shards(rows, cols, pair, ln_in_gain, proj_left, proj_right, gate_weight, ln_out_gain, out_weight):
    width = out_weight.shape[0]
    here_i, here_k = pair.shape[0], pair.shape[1]
    half, chips = here_i // 2, rows // 2
    both = ("row", "col")
    exchange = functools.partial(
        lax.all_to_all, axis_name=both, split_axis=0, concat_axis=0, tiled=True
    )
    gain = ln_in_gain.reshape(1, -1)
    sent = operands(pair, gain, proj_left, proj_right, chips, cols)
    got = exchange(sent.reshape(rows * cols, 2, half, here_k))
    got = got.reshape(rows, cols, 2, half, here_k)
    other = lax.ppermute(got[:, :, 1], "row", [(r, r ^ 1) for r in range(rows)])
    core = lax.rem(lax.axis_index("row"), 2).reshape(1)
    product = triangle(core, got, other)
    back = exchange(product.reshape(rows * cols, half, here_k))
    gate = gates(pair, gain, gate_weight)
    return updates(
        back.reshape(chips, 2, cols, half, here_k), ln_out_gain.reshape(width, 1), out_weight, gate
    )


def solution(mesh):
    rows, cols = mesh.shape["row"], mesh.shape["col"]
    in_specs = (P("row", "col", None), P(), P(), P(), P(), P(), P())
    out_specs = P("row", "col", None)
    step = functools.partial(shards, rows, cols)
    return jax.shard_map(step, mesh=mesh, in_specs=in_specs, out_specs=out_specs, check_vma=False)
```

time: 133 us -> 125 us (0.940)
  Pallas kernels: 0 us -> 12.5 us
  matrix products: 8.68 us -> 0 us
  other arithmetic: 6.7 us -> 0 us
  local copies, waits for them, and re-layouts: 11.2 us -> 5.21 us
    pallas_call x0 -> x4, Pallas kernels: none -> 12.5 us  [the longest x1 3.95 us: operands(): pl.pallas_call(operands_kernel, grid=(2,), in_specs=[pl.BlockSpec((half,...]
    dot_general x5 -> x0, matrix products: 8.68 us -> none  [the longest x2 3.02 us: gated_pair(): jnp.einsum('rcd,de->erc', normed, weights, preferred_element_type=jnp.flo...]
    reduce_sum x4 -> x0, other arithmetic: 4.45 us -> none  [the longest x2 2.61 us: layer_norm(): spread = jnp.mean(centered * centered, axis=dimension, keepdims=True)]
    reshape x2 -> x1, local copies, waits for them, and re-layouts: 2.39 us -> 0.11 us  [shards(): ln_out_gain.reshape(width, 1)]
    convert_element_type x3 -> x0, local copies, waits for them, and re-layouts: 2.21 us -> none  [the longest x2 1.95 us: gated_pair(): return (jax.nn.sigmoid(both[:width]) * both[width:]).astype(jnp.bfloat16)]
    convert_element_type x4 -> x0, other arithmetic: 1.69 us -> none  [the longest x2 1.11 us: gated_pair(): return (jax.nn.sigmoid(both[:width]) * both[width:]).astype(jnp.bfloat16)]
    transpose x2 -> x0, local copies, waits for them, and re-layouts: 1.47 us -> none  [by_device(): return jnp.swapaxes(side, 1, 2).reshape(rows * cols, half, here_k)]
    unnamed x20 -> x18, local copies, waits for them, and re-layouts: 3.16 us -> 3.58 us
  transfers between devices with their start and end apart: 2 -> 2, of which waited for: 2 -> 2; matrix products, arithmetic and copies ran while one was open for 2% -> 0% of each run, Pallas kernels for 0% -> 2%
where the time goes in v2:
time: 125 us; the launch traced here: 124 us
  blocking collectives  68.6 us (55%)
  waiting for transfers between devices  30.2 us (24%)
  Pallas kernels  12.5 us (10%)
  starting transfers between devices  7.65 us (6%)
  local copies, waits for them, and re-layouts  5.21 us (4%)
    all_to_all x1, blocking collectives, shards(): got = exchange(sent.reshape(rows * cols, 2, half, here_k))  68.6 us
    all_to_all x1, waiting for transfers between devices, shards(): back = exchange(product.reshape(rows * cols, half, here_k))  27.3 us
    all_to_all x1, starting transfers between devices, shards(): back = exchange(product.reshape(rows * cols, half, here_k))  7.65 us
    pallas_call x1, Pallas kernels, operands(): pl.pallas_call(operands_kernel, grid=(2,), in_specs=[pl.BlockSpec((half,...  3.95 us
    pallas_call x1, Pallas kernels, updates(): pl.pallas_call(update_kernel, grid=(2,), in_specs=[pl.BlockSpec((chips, 1...  3.74 us
    unnamed x18, local copies, waits for them, and re-layouts  3.58 us
    ppermute x1, waiting for transfers between devices, shards(): other = lax.ppermute(got[:, :, 1], 'row', [(r, r ^ 1) for r in range(rows)])  2.87 us
    pallas_call x1, Pallas kernels, triangle(): pl.pallas_call(triangle_kernel, in_specs=[pl.BlockSpec(memory_space=pltpu...  2.87 us
  transfers between devices with their start and end apart: 2, of which 2 were waited for; matrix products, arithmetic and copies ran while one was open for 0% of the time, Pallas kernels for 2%

profile of v2, /device:TPU:1, one launch (start us, length us, event | category | flops | bytes accessed | tf_op | source)
XLA Modules:
  0.0 124.2 jit_solution(3482821862051561266)
XLA Ops:
  0.0 0.0 copy-start
  0.0 1.2 copy-done
  1.2 0.0 copy-start.2
  1.2 0.8 copy-done.2
  2.1 0.0 copy-start.3
  2.1 0.8 copy-done.3
  2.9 0.0 copy-start.6
  2.9 0.7 copy-done.6
  3.6 3.9 %operands.1 = bf16[16,2,8,2,16,128]{5,4,3,2,1,0:T(8,128)(2,1)S(1)} custom-call(bf16[32,128,128]{2,1,0:T(8,128)(2,1)S(1)} %copy-done, f32[1,128]{1,0:T(1,128)S(1)} %bitcast.12, bf16[128,256]{1,0:T(8,128)(2,1)S(1)} %copy-done.2, bf16[128,256]{1,0:T(8,128)(2,1)S(1)} %copy-done.3), custom_call_target="tpu_custom_call" | custom-call | tf_op jit(solution)/shard_map/operands/pallas_call | solution.py:51
  7.5 68.6 %all_to_all.10 = bf16[256,2,16,128]{3,2,1,0:T(8,128)(2,1)S(1)} all-to-all(bf16[256,2,16,128]{3,2,1,0:T(8,128)(2,1)S(1)} %bitcast.11), channel_id=1, replica_groups=mesh['row'=32,'col'=8] {'row','col'}, dimensions={0} | all-to-all | bytes 4194304 | tf_op jit(solution)/shard_map/all_to_all | solution.py:182
  76.1 0.4 copy.11
  76.5 1.2 slice_bitcast_fusion
  77.6 0.0 collective-permute-start
  77.6 2.9 %collective-permute-done.other_ref = bf16[32,8,16,128]{3,2,1,0:T(8,128)(2,1)S(1)} collective-permute-done((bf16[32,8,16,128]{3,2,1,0:T(8,128)(2,1)}, bf16[32,8,16,128]{3,2,1,0:T(8,128)(2,1)S(1)}, u32[]{:S(2)}, u32[]{:S(2)}) %collective-permute-start) | collective-permute-done | bytes 1048608 | tf_op jit(solution)/shard_map/ppermute | solution.py:184
  80.5 2.9 %triangle.1 = bf16[32,8,16,128]{3,2,1,0:T(8,128)(2,1)} custom-call(s32[1]{0:T(128)} %bitcast.core_ref, bf16[32,8,2,16,128]{4,3,2,1,0:T(8,128)(2,1)S(1)} %bitcast.10, bf16[32,8,16,128]{3,2,1,0:T(8,128)(2,1)S(1)} %collective-permute-done.other_ref), custom_call_target="tpu_custom_call" | custom-call | tf_op jit(solution)/shard_map/triangle/pallas_call | solution.py:92
  83.4 0.0 copy-start.8
  83.4 0.0 copy-start.1
  83.4 0.0 copy-start.4
  83.4 0.0 copy-start.7
  83.4 7.6 %all-to-all-start.1 = ((bf16[256,16,128]{2,1,0:T(8,128)(2,1)}), bf16[256,16,128]{2,1,0:T(8,128)(2,1)}, u32[]{:S(2)}, u32[]{:S(2)}) async-start(bf16[256,16,128]{2,1,0:T(8,128)(2,1)} %bitcast.6), calls=%async_computation.1 | async-start | bytes 2097152 | tf_op jit(solution)/shard_map/all_to_all | solution.py:187
  91.0 0.0 copy-start.5
  91.0 0.0 copy-done.8
  91.1 0.1 copy.13.gain_ref
  91.2 0.0 copy-done.1
  91.2 0.0 copy-done.4
  91.2 0.0 copy-done.7
  91.2 2.0 %gates.1.gate_ref = f32[32,128,128]{2,1,0:T(8,128)S(1)} custom-call(bf16[32,128,128]{2,1,0:T(8,128)(2,1)S(1)} %copy-done.1, f32[1,128]{1,0:T(1,128)S(1)} %bitcast.13, bf16[128,128]{1,0:T(8,128)(2,1)S(1)} %copy-done.4), custom_call_target="tpu_custom_call" | custom-call | flops 134217728 | bytes 3145728 | tf_op jit(solution)/shard_map/gates/pallas_call | solution.py:118
  93.2 27.3 %all-to-all-done.1 = bf16[256,16,128]{2,1,0:T(8,128)(2,1)} async-done(((bf16[256,16,128]{2,1,0:T(8,128)(2,1)}), bf16[256,16,128]{2,1,0:T(8,128)(2,1)}, u32[]{:S(2)}, u32[]{:S(2)}) %all-to-all-start.1) | async-done | bytes 1048608 | tf_op jit(solution)/shard_map/all_to_all | solution.py:187
  120.5 0.0 copy-done.5
  120.5 3.7 %updates.1 = bf16[32,128,128]{2,1,0:T(8,128)(2,1)} custom-call(bf16[16,2,8,16,128]{4,3,2,1,0:T(8,128)(2,1)} %bitcast.7.back_ref, f32[128,1]{1,0:T(8,128)S(1)} %copy.13.gain_ref, bf16[128,128]{1,0:T(8,128)(2,1)S(1)} %copy-done.5, f32[32,128,128]{2,1,0:T(8,128)S(1)} %gates.1.gate_ref), custom_call_target="tpu_custom_call" | custom-call | tf_op jit(solution)/shard_map/updates/pallas_call | solution.py:156
Async XLA Ops:
  0.0 1.2 copy-start
  1.2 0.8 copy-start.2
  2.1 0.8 copy-start.3
  2.9 0.7 copy-start.6
  77.6 2.9 %collective-permute-start = (bf16[32,8,16,128]{3,2,1,0:T(8,128)(2,1)}, bf16[32,8,16,128]{3,2,1,0:T(8,128)(2,1)S(1)}, u32[]{:S(2)}, u32[]{:S(2)}) collective-permute-start(bf16[32,8,16,128]{3,2,1,0:T(8,128)(2,1)} %slice_bitcast_fusion), channel_id=1, source_target_pairs={{0,8},{8,0},{16,24},{24,16},{32,40},{40,32},{48,56},{56,48},{64,72... | collective-permute-start | bytes 3145736 | tf_op jit(solution)/shard_map/ppermute | solution.py:184
  83.4 7.7 %copy-start.8 = (f32[128]{0:T(128)S(1)}, f32[128]{0:T(128)}, u32[]{:S(2)}) copy-start(f32[128]{0:T(128)} %param.12) | copy-start | bytes 1540
  83.4 7.8 %copy-start.1 = (bf16[32,128,128]{2,1,0:T(8,128)(2,1)S(1)}, bf16[32,128,128]{2,1,0:T(8,128)(2,1)}, u32[]{:S(2)}) copy-start(bf16[32,128,128]{2,1,0:T(8,128)(2,1)} %pair_ref.3) | copy-start | bytes 3145732
  83.4 7.8 %copy-start.4 = (bf16[128,128]{1,0:T(8,128)(2,1)S(1)}, bf16[128,128]{1,0:T(8,128)(2,1)}, u32[]{:S(2)}) copy-start(bf16[128,128]{1,0:T(8,128)(2,1)} %weight_ref.2) | copy-start | bytes 98308
  83.4 7.8 %copy-start.7 = (f32[128]{0:T(128)S(1)}, f32[128]{0:T(128)}, u32[]{:S(2)}) copy-start(f32[128]{0:T(128)} %param.8) | copy-start | bytes 1540
  83.4 37.1 %all-to-all-start.1 = ((bf16[256,16,128]{2,1,0:T(8,128)(2,1)}), bf16[256,16,128]{2,1,0:T(8,128)(2,1)}, u32[]{:S(2)}, u32[]{:S(2)}) async-start(bf16[256,16,128]{2,1,0:T(8,128)(2,1)} %bitcast.6), calls=%async_computation.1 | async-start | bytes 2097152 | tf_op jit(solution)/shard_map/all_to_all | solution.py:187
  91.0 29.5 %copy-start.5 = (bf16[128,128]{1,0:T(8,128)(2,1)S(1)}, bf16[128,128]{1,0:T(8,128)(2,1)}, u32[]{:S(2)}) copy-start(bf16[128,128]{1,0:T(8,128)(2,1)} %weight_ref.3) | copy-start | bytes 98308

commit v3 on v2

v3 whole, which is shorter than its diff:
```python
import functools

import jax
import jax.numpy as jnp
from jax import lax
from jax.experimental import pallas as pl
from jax.experimental.pallas import tpu as pltpu
from jax.sharding import PartitionSpec as P

F32, BF16 = jnp.float32, jnp.bfloat16
VMEM_LIMIT = 40 * 1024 * 1024


def sigmoid(values):
    return 0.5 * jnp.tanh(0.5 * values) + 0.5


def normalize(values, gain):
    average = jnp.mean(values, axis=-1, keepdims=True)
    centered = values - average
    spread = jnp.mean(centered * centered, axis=-1, keepdims=True)
    return (centered * lax.rsqrt(spread + 1e-05) * gain).astype(BF16)


PARTS = 4


def operands_kernel(
    pair_hbm, gain_hbm, left_hbm, right_hbm, sent_ref, pair_ref, gain_ref, weights, turned, sides, arrived
):
    here_i, here_k, channels = pair_ref.shape
    chips, cores, cols, _, half, _ = sent_ref.shape
    wide = left_hbm.shape[1]
    width, part = wide // 2, here_i // PARTS
    pieces = [
        pltpu.make_async_copy(
            pair_hbm.at[pl.ds(p * part, part)], pair_ref.at[pl.ds(p * part, part)], arrived.at[p]
        )
        for p in range(PARTS)
    ]
    small = [
        pltpu.make_async_copy(left_hbm, weights.at[0], arrived.at[PARTS]),
        pltpu.make_async_copy(right_hbm, weights.at[1], arrived.at[PARTS + 1]),
        pltpu.make_async_copy(gain_hbm, gain_ref, arrived.at[PARTS + 2]),
    ]
    for copy in pieces[:1] + small + pieces[1:]:
        copy.start()
    for copy in small:
        copy.wait()
    for side in range(2):
        turned[side * wide : (side + 1) * wide] = weights[side].astype(F32).T.astype(BF16)
    gain = gain_ref[...]
    for core in range(cores):
        for i in range(0, half, 2):
            row = core * half + i
            if row % part == 0:
                pieces[row // part].wait()
            rows = pair_ref[row : row + 2].reshape(2 * here_k, channels).astype(F32)
            normed = normalize(rows, gain)
            both = lax.dot_general(
                turned[...], normed, (((1,), (1,)), ((), ())), preferred_element_type=F32
            )
            for side in range(2):
                one = both[side * wide : (side + 1) * wide]
                gated = sigmoid(one[:width]) * one[width:]
                sides[core, side, i] = gated[:, :here_k]
                sides[core, side, i + 1] = gated[:, here_k:]
        for side in range(2):
            by_channel = jnp.swapaxes(sides[core, side], 0, 1).astype(BF16)
            sent_ref[:, core, :, side] = by_channel.reshape(chips, cols, half, here_k)


def operands(pair, gain, proj_left, proj_right, chips, cols):
    here_i, here_k, channels = pair.shape
    half, wide = here_i // 2, proj_left.shape[1]
    hbm = pl.BlockSpec(memory_space=pltpu.HBM)
    arrays = [
        pltpu.with_memory_space_constraint(array, pltpu.HBM)
        for array in (pair, gain, proj_left, proj_right)
    ]
    return pl.pallas_call(
        operands_kernel,
        in_specs=[hbm] * 4,
        out_specs=pl.BlockSpec(memory_space=pltpu.VMEM),
        out_shape=jax.ShapeDtypeStruct((chips, 2, cols, 2, half, here_k), BF16),
        scratch_shapes=[
            pltpu.VMEM(pair.shape, BF16),
            pltpu.VMEM(gain.shape, F32),
            pltpu.VMEM((2, channels, wide), BF16),
            pltpu.VMEM((2 * wide, channels), BF16),
            pltpu.VMEM((2, 2, half, wide // 2, here_k), F32),
            pltpu.SemaphoreType.DMA((PARTS + 3,)),
        ],
        compiler_params=pltpu.CompilerParams(vmem_limit_bytes=VMEM_LIMIT),
        name="operands",
    )(*arrays)


def split_kernel(got_ref, right_ref):
    right_ref[...] = got_ref[:, :, 1]


def split(got):
    rows, cols, _, half, here_k = got.shape
    vmem = pl.BlockSpec(memory_space=pltpu.VMEM)
    return pl.pallas_call(
        split_kernel,
        in_specs=[vmem],
        out_specs=vmem,
        out_shape=jax.ShapeDtypeStruct((rows, cols, half, here_k), BF16),
        compiler_params=pltpu.CompilerParams(vmem_limit_bytes=VMEM_LIMIT),
        name="split",
    )(got)


def own_kernel(got_ref, left_ref, own_ref, right):
    rows, cols, _, half, here_k = got_ref.shape
    for s in range(cols):
        span = pl.ds(s * here_k, here_k)
        left_ref[:, span] = got_ref[:, s, 0].reshape(rows * half, here_k)
        right[:, span] = got_ref[:, s, 1].reshape(rows * half, here_k)
    step = 2 * here_k
    for j in range(0, rows * half, step):
        own_ref[:, j : j + step] = lax.dot_general(
            left_ref[...], right[j : j + step], (((1,), (1,)), ((), ())), preferred_element_type=F32
        ).astype(BF16)


def own_part(got):
    rows, cols, _, half, here_k = got.shape
    tall, deep = rows * half, cols * here_k
    vmem = pl.BlockSpec(memory_space=pltpu.VMEM)
    return pl.pallas_call(
        own_kernel,
        in_specs=[vmem],
        out_specs=[vmem, vmem],
        out_shape=[
            jax.ShapeDtypeStruct((tall, deep), BF16),
            jax.ShapeDtypeStruct((tall, tall), BF16),
        ],
        scratch_shapes=[pltpu.VMEM((tall, deep), BF16)],
        compiler_params=pltpu.CompilerParams(vmem_limit_bytes=VMEM_LIMIT),
        cost_estimate=pl.CostEstimate(
            flops=2 * tall * tall * deep, bytes_accessed=8 * tall * deep, transcendentals=0
        ),
        name="own_part",
    )(got)


def merge_kernel(left_ref, own_ref, other_ref, product_ref, right):
    rows, cols, half, here_k = other_ref.shape
    each = rows // cols * half
    for s in range(cols):
        span = pl.ds(s * here_k, here_k)
        block = other_ref[:, s].reshape(cols // 2, 2, each, here_k)
        right[:, 1, :, span] = block[:, 0]
        right[:, 0, :, span] = block[:, 1]
    first = lax.broadcasted_iota(jnp.int32, (1, here_k), 1) < each
    for pair in range(0, cols // 2, 2):
        part = right[pair : pair + 2].reshape(2 * here_k, cols * here_k)
        total = lax.dot_general(
            left_ref[...], part, (((1,), (1,)), ((), ())), preferred_element_type=F32
        )
        for p in range(2):
            span = pl.ds((pair + p) * here_k, here_k)
            own = own_ref[:, span].astype(F32)
            other = total[:, p * here_k : (p + 1) * here_k]
            even = jnp.where(first, own, other).astype(BF16)
            odd = jnp.where(first, other, own).astype(BF16)
            product_ref[:, 2 * (pair + p)] = even.reshape(rows, half, here_k)
            product_ref[:, 2 * (pair + p) + 1] = odd.reshape(rows, half, here_k)


def merge(left, own, other):
    rows, cols, half, here_k = other.shape
    vmem = pl.BlockSpec(memory_space=pltpu.VMEM)
    return pl.pallas_call(
        merge_kernel,
        in_specs=[vmem, vmem, vmem],
        out_specs=vmem,
        out_shape=jax.ShapeDtypeStruct(other.shape, BF16),
        scratch_shapes=[
            pltpu.VMEM((cols // 2, 2, rows // cols * half, cols * here_k), BF16),
        ],
        compiler_params=pltpu.CompilerParams(vmem_limit_bytes=VMEM_LIMIT),
        name="merge",
    )(left, own, other)


def gate_kernel(pair_ref, gain_ref, weight_ref, gate_ref):
    some, here_k, channels = pair_ref.shape
    rows = pair_ref[...].reshape(some * here_k, channels).astype(F32)
    normed = normalize(rows, gain_ref[...])
    gate = sigmoid(jnp.dot(normed, weight_ref[...], preferred_element_type=F32))
    gate_ref[...] = gate.reshape(gate_ref.shape)


def gates(pair, gain, weight):
    here_i, here_k, channels = pair.shape
    some = here_i // 4
    block = pl.BlockSpec((some, here_k, channels), lambda i: (i, 0, 0))
    return pl.pallas_call(
        gate_kernel,
        grid=(4,),
        in_specs=[
            block,
            pl.BlockSpec(gain.shape, lambda i: (0, 0)),
            pl.BlockSpec(weight.shape, lambda i: (0, 0)),
        ],
        out_specs=block,
        out_shape=jax.ShapeDtypeStruct(pair.shape, F32),
        compiler_params=pltpu.CompilerParams(vmem_limit_bytes=VMEM_LIMIT),
        cost_estimate=pl.CostEstimate(
            flops=2 * pair.size * channels, bytes_accessed=6 * pair.size, transcendentals=pair.size
        ),
        name="gates",
    )(pair, gain, weight)


def update_kernel(
    odd_ref, back_hbm, gain_ref, weight_ref, gate_ref, update_hbm, back_ref, update_ref, arrived, left
):
    chips, cores, cols, half, here_k = back_ref.shape
    width, each = chips * cols, gate_ref.shape[1]
    channels = gate_ref.shape[4]
    odd = odd_ref[0]
    incoming = [
        pltpu.make_async_copy(back_hbm.at[:, c], back_ref.at[:, c], arrived.at[c])
        for c in range(cores)
    ]
    for copy in incoming:
        copy.start()
    gain = jnp.broadcast_to(gain_ref[...], (here_k, width)).T
    outgoing = []
    for c in range(cores):
        incoming[c].wait()
        product = back_ref[:, c].reshape(width, half, here_k).astype(F32)
        average = jnp.mean(product, axis=0, keepdims=True)
        centered = product - average
        spread = jnp.mean(centered * centered, axis=0, keepdims=True)
        normed = centered * lax.rsqrt(spread + 1e-05)
        normed = (jnp.swapaxes(normed, 0, 1) * gain).astype(BF16)
        first = (c + odd) % 2
        for i in range(half):
            row = c * half + i
            projected = lax.dot_general(
                normed[i], weight_ref[...], (((0,), (0,)), ((), ())), preferred_element_type=F32
            ).reshape(2, each, half, channels)
            update_ref[row, :, first] = (gate_ref[row, :, first] * projected[0]).astype(BF16)
            second = 1 - first
            update_ref[row, :, second] = (gate_ref[row, :, second] * projected[1]).astype(BF16)
            if (i + 1) % 4 == 0:
                span = pl.ds(row - 3, 4)
                copy = pltpu.make_async_copy(
                    update_ref.at[span], update_hbm.at[span], left.at[len(outgoing)]
                )
                copy.start()
                outgoing.append(copy)
    for copy in outgoing:
        copy.wait()


def updates(odd, back, gain, weight, gate):
    chips, _, cols, half, here_k = back.shape
    here_i, _, channels = gate.shape
    blocked = (here_i, here_k // (2 * half), 2, half, channels)
    vmem, hbm = pl.BlockSpec(memory_space=pltpu.VMEM), pl.BlockSpec(memory_space=pltpu.HBM)
    update = pl.pallas_call(
        update_kernel,
        in_specs=[pl.BlockSpec(memory_space=pltpu.SMEM), hbm, vmem, vmem, vmem],
        out_specs=hbm,
        out_shape=jax.ShapeDtypeStruct(blocked, BF16),
        scratch_shapes=[
            pltpu.VMEM(back.shape, BF16),
            pltpu.VMEM(blocked, BF16),
            pltpu.SemaphoreType.DMA((2,)),
            pltpu.SemaphoreType.DMA((here_i // 4,)),
        ],
        compiler_params=pltpu.CompilerParams(vmem_limit_bytes=VMEM_LIMIT),
        name="updates",
    )(odd, back, gain, weight, gate.reshape(blocked))
    return update.reshape(gate.shape)


def shards(rows, cols, pair, ln_in_gain, proj_left, proj_right, gate_weight, ln_out_gain, out_weight):
    width = out_weight.shape[0]
    here_i, here_k = pair.shape[0], pair.shape[1]
    half, chips = here_i // 2, rows // 2
    both = ("row", "col")
    exchange = functools.partial(
        lax.all_to_all, axis_name=both, split_axis=0, concat_axis=0, tiled=True
    )
    gain = ln_in_gain.reshape(1, -1)
    sent = operands(pair, gain, proj_left, proj_right, chips, cols)
    got = exchange(sent.reshape(rows * cols, 2, half, here_k))
    got = got.reshape(rows, cols, 2, half, here_k)
    other = lax.ppermute(split(got), "row", [(r, r ^ 1) for r in range(rows)])
    left, own = own_part(got)
    product = merge(left, own, other)
    product, late_pair = lax.optimization_barrier((product, pair))
    back = exchange(product.reshape(rows * cols, half, here_k))
    gate = gates(late_pair, gain, gate_weight)
    odd = lax.rem(lax.axis_index("col"), 2).reshape(1)
    return updates(
        odd, back.reshape(chips, 2, cols, half, here_k), ln_out_gain.reshape(1, width), out_weight, gate
    )


def solution(mesh):
    rows, cols = mesh.shape["row"], mesh.shape["col"]
    in_specs = (P("row", "col", None), P(), P(), P(), P(), P(), P())
    out_specs = P("row", "col", None)
    step = functools.partial(shards, rows, cols)
    return jax.shard_map(step, mesh=mesh, in_specs=in_specs, out_specs=out_specs, check_vma=False)
```

time: 125 us -> 118 us (0.944)
  local copies, waits for them, and re-layouts: 5.21 us -> 1.24 us
  waiting for transfers between devices: 30.2 us -> 28.9 us
    unnamed x18 -> x10, local copies, waits for them, and re-layouts: 3.58 us -> 1.24 us
    pallas_call x3 -> x5, Pallas kernels: 10.5 us -> 9.91 us  [the longest x1 4.45 us: operands(): pl.pallas_call(operands_kernel, in_specs=[hbm] * 4, out_specs=pl.BlockSpe...]
where the time goes in v3:
time: 118 us; the launch traced here: 117 us
  blocking collectives  68.6 us (58%)
  waiting for transfers between devices  28.9 us (24%)
  Pallas kernels  11.9 us (10%)
  starting transfers between devices  6.74 us (6%)
  local copies, waits for them, and re-layouts  1.24 us (1%)
    all_to_all x1, blocking collectives, shards(): got = exchange(sent.reshape(rows * cols, 2, half, here_k))  68.6 us
    all_to_all x1, waiting for transfers between devices, shards(): back = exchange(product.reshape(rows * cols, half, here_k))  27.1 us
    all_to_all x1, starting transfers between devices, shards(): back = exchange(product.reshape(rows * cols, half, here_k))  6.65 us
    pallas_call x1, Pallas kernels, operands(): pl.pallas_call(operands_kernel, in_specs=[hbm] * 4, out_specs=pl.BlockSpe...  4.45 us
    pallas_call x1, Pallas kernels, updates(): pl.pallas_call(update_kernel, in_specs=[pl.BlockSpec(memory_space=pltpu.S...  2.81 us
  transfers between devices with their start and end apart: 2, of which 2 were waited for; matrix products, arithmetic and copies ran while one was open for 0% of the time, Pallas kernels for 2%

profile of v3, /device:TPU:1, one launch (start us, length us, event | category | flops | bytes accessed | tf_op | source)
XLA Modules:
  0.0 117.5 jit_solution(3706817599053269692)
XLA Ops:
  0.0 4.4 %operands.1 = bf16[16,2,8,2,16,128]{5,4,3,2,1,0:T(8,128)(2,1)S(1)} custom-call(bf16[32,128,128]{2,1,0:T(8,128)(2,1)} %pair_ref, f32[1,128]{1,0:T(1,128)} %bitcast.14, bf16[128,256]{1,0:T(8,128)(2,1)} %left_hbm.1, bf16[128,256]{1,0:T(8,128)(2,1)} %right_hbm.1), custom_call_target="tpu_custom_call" | custom-call | tf_op jit(solution)/shard_map/operands/pallas_call | solution.py:81
  4.5 68.6 %all_to_all.10 = bf16[256,2,16,128]{3,2,1,0:T(8,128)(2,1)S(1)} all-to-all(bf16[256,2,16,128]{3,2,1,0:T(8,128)(2,1)S(1)} %bitcast.12), channel_id=1, replica_groups=mesh['row'=32,'col'=8] {'row','col'}, dimensions={0} | all-to-all | bytes 4194304 | tf_op jit(solution)/shard_map/all_to_all | solution.py:295
  73.0 0.1 split.1
  73.1 0.1 collective-permute-start
  73.2 0.8 own_part.1
  74.0 1.8 %collective-permute-done.other_ref = bf16[32,8,16,128]{3,2,1,0:T(8,128)(2,1)S(1)} collective-permute-done((bf16[32,8,16,128]{3,2,1,0:T(8,128)(2,1)S(1)}, bf16[32,8,16,128]{3,2,1,0:T(8,128)(2,1)S(1)}, u32[]{:S(2)}, u32[]{:S(2)}) %collective-permute-start) | collective-permute-done | bytes 1048608 | tf_op jit(solution)/shard_map/ppermute | solution.py:297
  75.9 0.0 copy-start.1
  75.9 0.0 copy-start.3
  75.9 1.8 %merge.1 = bf16[32,8,16,128]{3,2,1,0:T(8,128)(2,1)} custom-call(bf16[512,1024]{1,0:T(8,128)(2,1)S(1)} %get-tuple-element.9.left_ref, bf16[512,512]{1,0:T(8,128)(2,1)S(1)} %get-tuple-element.10.own_ref, bf16[32,8,16,128]{3,2,1,0:T(8,128)(2,1)S(1)} %collective-permute-done.other_ref), custom_call_target="tpu_custom_call" | custom-call | tf_op jit(solution)/shard_map/merge/pallas_call | solution.py:177
  77.6 0.0 copy-start.2
  77.6 6.6 %all-to-all-start.1 = ((bf16[256,16,128]{2,1,0:T(8,128)(2,1)}), bf16[256,16,128]{2,1,0:T(8,128)(2,1)S(1)}, u32[]{:S(2)}, u32[]{:S(2)}) async-start(bf16[256,16,128]{2,1,0:T(8,128)(2,1)} %bitcast.4), calls=%async_computation.1 | async-start | bytes 2097152 | tf_op jit(solution)/shard_map/all_to_all | solution.py:301
  84.3 0.0 copy-start.4
  84.3 0.0 copy-done.1
  84.3 0.0 copy-done.3
  84.3 0.0 copy-start
  84.3 1.2 %copy-done = bf16[32,128,128]{2,1,0:T(8,128)(2,1)S(1)} copy-done((bf16[32,128,128]{2,1,0:T(8,128)(2,1)S(1)}, bf16[32,128,128]{2,1,0:T(8,128)(2,1)}, u32[]{:S(2)}) %copy-start) | copy-done | bytes 1048600
  85.6 2.0 %gates.1 = f32[32,128,128]{2,1,0:T(8,128)S(1)} custom-call(bf16[32,128,128]{2,1,0:T(8,128)(2,1)S(1)} %copy-done, f32[1,128]{1,0:T(1,128)S(1)} %bitcast.15, bf16[128,128]{1,0:T(8,128)(2,1)S(1)} %copy-done.1), custom_call_target="tpu_custom_call" | custom-call | flops 134217728 | bytes 3145728 | tf_op jit(solution)/shard_map/gates/pallas_call | solution.py:202
  87.5 27.1 %all-to-all-done.1 = bf16[256,16,128]{2,1,0:T(8,128)(2,1)S(1)} async-done(((bf16[256,16,128]{2,1,0:T(8,128)(2,1)}), bf16[256,16,128]{2,1,0:T(8,128)(2,1)S(1)}, u32[]{:S(2)}, u32[]{:S(2)}) %all-to-all-start.1) | async-done | bytes 1048608 | tf_op jit(solution)/shard_map/all_to_all | solution.py:301
  114.6 0.0 copy-done.2
  114.6 0.0 copy-done.4
  114.6 2.8 %updates.1 = bf16[32,4,2,16,128]{4,3,2,1,0:T(8,128)(2,1)} custom-call(s32[1]{0:T(128)} %bitcast.odd_ref, bf16[16,2,8,16,128]{4,3,2,1,0:T(8,128)(2,1)S(1)} %bitcast.13, f32[1,128]{1,0:T(1,128)S(1)} %bitcast.16, bf16[128,128]{1,0:T(8,128)(2,1)S(1)} %copy-done.2, f32[32,4,2,16,128]{4,3,2,1,0:T(8,128)S(1)} %bitcast.11), custom_call_target="tpu_custom_call" | custom-call | tf_op jit(solution)/shard_map/updates/pallas_call | solution.py:268
Async XLA Ops:
  73.1 2.7 %collective-permute-start = (bf16[32,8,16,128]{3,2,1,0:T(8,128)(2,1)S(1)}, bf16[32,8,16,128]{3,2,1,0:T(8,128)(2,1)S(1)}, u32[]{:S(2)}, u32[]{:S(2)}) collective-permute-start(bf16[32,8,16,128]{3,2,1,0:T(8,128)(2,1)S(1)} %split.1), channel_id=1, source_target_pairs={{0,8},{8,0},{16,24},{24,16},{32,40},{40,32},{48,56},{56,48},{64,72... | collective-permute-start | bytes 3145736 | tf_op jit(solution)/shard_map/ppermute | solution.py:297
  75.9 8.5 %copy-start.1 = (bf16[128,128]{1,0:T(8,128)(2,1)S(1)}, bf16[128,128]{1,0:T(8,128)(2,1)}, u32[]{:S(2)}) copy-start(bf16[128,128]{1,0:T(8,128)(2,1)} %weight_ref.2) | copy-start | bytes 98308
  75.9 8.5 %copy-start.3 = (f32[128]{0:T(128)S(1)}, f32[128]{0:T(128)}, u32[]{:S(2)}) copy-start(f32[128]{0:T(128)} %param.8) | copy-start | bytes 1540
  77.6 37.0 %copy-start.2 = (bf16[128,128]{1,0:T(8,128)(2,1)S(1)}, bf16[128,128]{1,0:T(8,128)(2,1)}, u32[]{:S(2)}) copy-start(bf16[128,128]{1,0:T(8,128)(2,1)} %weight_ref.3) | copy-start | bytes 98308
  77.6 37.0 %all-to-all-start.1 = ((bf16[256,16,128]{2,1,0:T(8,128)(2,1)}), bf16[256,16,128]{2,1,0:T(8,128)(2,1)S(1)}, u32[]{:S(2)}, u32[]{:S(2)}) async-start(bf16[256,16,128]{2,1,0:T(8,128)(2,1)} %bitcast.4), calls=%async_computation.1 | async-start | bytes 2097152 | tf_op jit(solution)/shard_map/all_to_all | solution.py:301
  84.3 30.4 %copy-start.4 = (f32[128]{0:T(128)S(1)}, f32[128]{0:T(128)}, u32[]{:S(2)}) copy-start(f32[128]{0:T(128)} %param.12) | copy-start | bytes 1540
  84.3 1.2 %copy-start = (bf16[32,128,128]{2,1,0:T(8,128)(2,1)S(1)}, bf16[32,128,128]{2,1,0:T(8,128)(2,1)}, u32[]{:S(2)}) copy-start(bf16[32,128,128]{2,1,0:T(8,128)(2,1)} %pair_ref) | copy-start | bytes 3145732

commit v4 on v3

--- a/solution.py
+++ b/solution.py
@@ -48,7 +48,7 @@
     for copy in small:
         copy.wait()
     for side in range(2):
-        turned[side * wide : (side + 1) * wide] = weights[side].astype(F32).T.astype(BF16)
+        turned[side * wide : (side + 1) * wide] = (0.5 * weights[side].astype(F32)).T.astype(BF16)
     gain = gain_ref[...]
     for core in range(cores):
         for i in range(0, half, 2):
@@ -62,7 +62,7 @@
             )
             for side in range(2):
                 one = both[side * wide : (side + 1) * wide]
-                gated = sigmoid(one[:width]) * one[width:]
+                gated = (jnp.tanh(one[:width]) + 1.0) * one[width:]
                 sides[core, side, i] = gated[:, :here_k]
                 sides[core, side, i + 1] = gated[:, here_k:]
         for side in range(2):
@@ -147,7 +147,7 @@
     )(got)
 
 
-def merge_kernel(left_ref, own_ref, other_ref, product_ref, right):
+def merge_kernel(left_ref, own_ref, other_ref, product_hbm, product_ref, right, left):
     rows, cols, half, here_k = other_ref.shape
     each = rows // cols * half
     for s in range(cols):
@@ -155,6 +155,7 @@
         block = other_ref[:, s].reshape(cols // 2, 2, each, here_k)
         right[:, 1, :, span] = block[:, 0]
         right[:, 0, :, span] = block[:, 1]
+    outgoing = []
     first = lax.broadcasted_iota(jnp.int32, (1, here_k), 1) < each
     for pair in range(0, cols // 2, 2):
         part = right[pair : pair + 2].reshape(2 * here_k, cols * here_k)
@@ -169,6 +170,14 @@
             odd = jnp.where(first, other, own).astype(BF16)
             product_ref[:, 2 * (pair + p)] = even.reshape(rows, half, here_k)
             product_ref[:, 2 * (pair + p) + 1] = odd.reshape(rows, half, here_k)
+            span = pl.ds(2 * (pair + p), 2)
+            copy = pltpu.make_async_copy(
+                product_ref.at[:, span], product_hbm.at[:, span], left.at[pair + p]
+            )
+            copy.start()
+            outgoing.append(copy)
+    for copy in outgoing:
+        copy.wait()
 
 
 def merge(left, own, other):
@@ -177,10 +186,12 @@
     return pl.pallas_call(
         merge_kernel,
         in_specs=[vmem, vmem, vmem],
-        out_specs=vmem,
+        out_specs=pl.BlockSpec(memory_space=pltpu.HBM),
         out_shape=jax.ShapeDtypeStruct(other.shape, BF16),
         scratch_shapes=[
+            pltpu.VMEM(other.shape, BF16),
             pltpu.VMEM((cols // 2, 2, rows // cols * half, cols * here_k), BF16),
+            pltpu.SemaphoreType.DMA((cols // 2,)),
         ],
         compiler_params=pltpu.CompilerParams(vmem_limit_bytes=VMEM_LIMIT),
         name="merge",
@@ -218,22 +229,15 @@
 
 
 def update_kernel(
-    odd_ref, back_hbm, gain_ref, weight_ref, gate_ref, update_hbm, back_ref, update_ref, arrived, left
+    odd_ref, back_ref, gain_ref, weight_ref, gate_ref, update_hbm, update_ref, left
 ):
     chips, cores, cols, half, here_k = back_ref.shape
     width, each = chips * cols, gate_ref.shape[1]
     channels = gate_ref.shape[4]
     odd = odd_ref[0]
-    incoming = [
-        pltpu.make_async_copy(back_hbm.at[:, c], back_ref.at[:, c], arrived.at[c])
-        for c in range(cores)
-    ]
-    for copy in incoming:
-        copy.start()
     gain = jnp.broadcast_to(gain_ref[...], (here_k, width)).T
     outgoing = []
     for c in range(cores):
-        incoming[c].wait()
         product = back_ref[:, c].reshape(width, half, here_k).astype(F32)
         average = jnp.mean(product, axis=0, keepdims=True)
         centered = product - average
@@ -267,13 +271,11 @@
     vmem, hbm = pl.BlockSpec(memory_space=pltpu.VMEM), pl.BlockSpec(memory_space=pltpu.HBM)
     update = pl.pallas_call(
         update_kernel,
-        in_specs=[pl.BlockSpec(memory_space=pltpu.SMEM), hbm, vmem, vmem, vmem],
+        in_specs=[pl.BlockSpec(memory_space=pltpu.SMEM), vmem, vmem, vmem, vmem],
         out_specs=hbm,
         out_shape=jax.ShapeDtypeStruct(blocked, BF16),
         scratch_shapes=[
-            pltpu.VMEM(back.shape, BF16),
             pltpu.VMEM(blocked, BF16),
-            pltpu.SemaphoreType.DMA((2,)),
             pltpu.SemaphoreType.DMA((here_i // 4,)),
         ],
         compiler_params=pltpu.CompilerParams(vmem_limit_bytes=VMEM_LIMIT),

time: 118 us -> 117 us (level)
  no operation moved by 1% of the time
where the time goes in v4:
time: 117 us
  blocking collectives  68.6 us (59%)
  waiting for transfers between devices  28.9 us (25%)
  Pallas kernels  11.4 us (10%)
  starting transfers between devices  6.74 us (6%)
  local copies, waits for them, and re-layouts  1.24 us (1%)
    all_to_all x1, blocking collectives, shards(): got = exchange(sent.reshape(rows * cols, 2, half, here_k))  68.6 us
    all_to_all x1, waiting for transfers between devices, shards(): back = exchange(product.reshape(rows * cols, half, here_k))  27.1 us
    all_to_all x1, starting transfers between devices, shards(): back = exchange(product.reshape(rows * cols, half, here_k))  6.65 us
    pallas_call x1, Pallas kernels, operands(): pl.pallas_call(operands_kernel, in_specs=[hbm] * 4, out_specs=pl.BlockSpe...  4.37 us
    pallas_call x1, Pallas kernels, updates(): pl.pallas_call(update_kernel, in_specs=[pl.BlockSpec(memory_space=pltpu.S...  2.39 us
  transfers between devices with their start and end apart: 2, of which 2 were waited for; matrix products, arithmetic and copies ran while one was open for 0% of the time, Pallas kernels for 2%

profile of v4, /device:TPU:1, one launch (start us, length us, event | category | flops | bytes accessed | tf_op | source)
XLA Modules:
  0.0 117.0 jit_solution(16998604060916298970)
XLA Ops:
  0.0 4.4 %operands.1 = bf16[16,2,8,2,16,128]{5,4,3,2,1,0:T(8,128)(2,1)S(1)} custom-call(bf16[32,128,128]{2,1,0:T(8,128)(2,1)} %pair_ref, f32[1,128]{1,0:T(1,128)} %bitcast.14, bf16[128,256]{1,0:T(8,128)(2,1)} %left_hbm.1, bf16[128,256]{1,0:T(8,128)(2,1)} %right_hbm.1), custom_call_target="tpu_custom_call" | custom-call | tf_op jit(solution)/shard_map/operands/pallas_call | solution.py:81
  4.4 68.6 %all_to_all.10 = bf16[256,2,16,128]{3,2,1,0:T(8,128)(2,1)S(1)} all-to-all(bf16[256,2,16,128]{3,2,1,0:T(8,128)(2,1)S(1)} %bitcast.12), channel_id=1, replica_groups=mesh['row'=32,'col'=8] {'row','col'}, dimensions={0} | all-to-all | bytes 4194304 | tf_op jit(solution)/shard_map/all_to_all | solution.py:297
  73.0 0.1 split.1
  73.0 0.1 collective-permute-start
  73.1 0.8 own_part.1
  74.0 1.8 %collective-permute-done.other_ref = bf16[32,8,16,128]{3,2,1,0:T(8,128)(2,1)S(1)} collective-permute-done((bf16[32,8,16,128]{3,2,1,0:T(8,128)(2,1)S(1)}, bf16[32,8,16,128]{3,2,1,0:T(8,128)(2,1)S(1)}, u32[]{:S(2)}, u32[]{:S(2)}) %collective-permute-start) | collective-permute-done | bytes 1048608 | tf_op jit(solution)/shard_map/ppermute | solution.py:299
  75.8 0.0 copy-start.1
  75.8 0.0 copy-start.3
  75.8 1.8 %merge.1 = bf16[32,8,16,128]{3,2,1,0:T(8,128)(2,1)} custom-call(bf16[512,1024]{1,0:T(8,128)(2,1)S(1)} %get-tuple-element.9.left_ref, bf16[512,512]{1,0:T(8,128)(2,1)S(1)} %get-tuple-element.10.own_ref, bf16[32,8,16,128]{3,2,1,0:T(8,128)(2,1)S(1)} %collective-permute-done.other_ref), custom_call_target="tpu_custom_call" | custom-call | tf_op jit(solution)/shard_map/merge/pallas_call | solution.py:186
  77.6 0.0 copy-start.2
  77.6 6.7 %all-to-all-start.1 = ((bf16[256,16,128]{2,1,0:T(8,128)(2,1)}), bf16[256,16,128]{2,1,0:T(8,128)(2,1)S(1)}, u32[]{:S(2)}, u32[]{:S(2)}) async-start(bf16[256,16,128]{2,1,0:T(8,128)(2,1)} %bitcast.4), calls=%async_computation.1 | async-start | bytes 2097152 | tf_op jit(solution)/shard_map/all_to_all | solution.py:303
  84.3 0.0 copy-start.4
  84.3 0.0 copy-done.1
  84.3 0.0 copy-done.3
  84.3 0.0 copy-start
  84.3 1.2 %copy-done = bf16[32,128,128]{2,1,0:T(8,128)(2,1)S(1)} copy-done((bf16[32,128,128]{2,1,0:T(8,128)(2,1)S(1)}, bf16[32,128,128]{2,1,0:T(8,128)(2,1)}, u32[]{:S(2)}) %copy-start) | copy-done | bytes 1048600
  85.5 2.0 %gates.1 = f32[32,128,128]{2,1,0:T(8,128)S(1)} custom-call(bf16[32,128,128]{2,1,0:T(8,128)(2,1)S(1)} %copy-done, f32[1,128]{1,0:T(1,128)S(1)} %bitcast.15, bf16[128,128]{1,0:T(8,128)(2,1)S(1)} %copy-done.1), custom_call_target="tpu_custom_call" | custom-call | flops 134217728 | bytes 3145728 | tf_op jit(solution)/shard_map/gates/pallas_call | solution.py:213
  87.5 27.1 %all-to-all-done.1 = bf16[256,16,128]{2,1,0:T(8,128)(2,1)S(1)} async-done(((bf16[256,16,128]{2,1,0:T(8,128)(2,1)}), bf16[256,16,128]{2,1,0:T(8,128)(2,1)S(1)}, u32[]{:S(2)}, u32[]{:S(2)}) %all-to-all-start.1) | async-done | bytes 1048608 | tf_op jit(solution)/shard_map/all_to_all | solution.py:303
  114.6 0.0 copy-done.2
  114.6 0.0 copy-done.4
  114.6 2.4 %updates.1 = bf16[32,4,2,16,128]{4,3,2,1,0:T(8,128)(2,1)} custom-call(s32[1]{0:T(128)} %bitcast.odd_ref, bf16[16,2,8,16,128]{4,3,2,1,0:T(8,128)(2,1)S(1)} %bitcast.13, f32[1,128]{1,0:T(1,128)S(1)} %bitcast.16, bf16[128,128]{1,0:T(8,128)(2,1)S(1)} %copy-done.2, f32[32,4,2,16,128]{4,3,2,1,0:T(8,128)S(1)} %bitcast.11), custom_call_target="tpu_custom_call" | custom-call | tf_op jit(solution)/shard_map/updates/pallas_call | solution.py:272
Async XLA Ops:
  73.0 2.7 %collective-permute-start = (bf16[32,8,16,128]{3,2,1,0:T(8,128)(2,1)S(1)}, bf16[32,8,16,128]{3,2,1,0:T(8,128)(2,1)S(1)}, u32[]{:S(2)}, u32[]{:S(2)}) collective-permute-start(bf16[32,8,16,128]{3,2,1,0:T(8,128)(2,1)S(1)} %split.1), channel_id=1, source_target_pairs={{0,8},{8,0},{16,24},{24,16},{32,40},{40,32},{48,56},{56,48},{64,72... | collective-permute-start | bytes 3145736 | tf_op jit(solution)/shard_map/ppermute | solution.py:299
  75.8 8.5 %copy-start.1 = (bf16[128,128]{1,0:T(8,128)(2,1)S(1)}, bf16[128,128]{1,0:T(8,128)(2,1)}, u32[]{:S(2)}) copy-start(bf16[128,128]{1,0:T(8,128)(2,1)} %weight_ref.2) | copy-start | bytes 98308
  75.8 8.5 %copy-start.3 = (f32[128]{0:T(128)S(1)}, f32[128]{0:T(128)}, u32[]{:S(2)}) copy-start(f32[128]{0:T(128)} %param.8) | copy-start | bytes 1540
  77.6 37.0 %copy-start.2 = (bf16[128,128]{1,0:T(8,128)(2,1)S(1)}, bf16[128,128]{1,0:T(8,128)(2,1)}, u32[]{:S(2)}) copy-start(bf16[128,128]{1,0:T(8,128)(2,1)} %weight_ref.3) | copy-start | bytes 98308
  77.6 37.0 %all-to-all-start.1 = ((bf16[256,16,128]{2,1,0:T(8,128)(2,1)}), bf16[256,16,128]{2,1,0:T(8,128)(2,1)S(1)}, u32[]{:S(2)}, u32[]{:S(2)}) async-start(bf16[256,16,128]{2,1,0:T(8,128)(2,1)} %bitcast.4), calls=%async_computation.1 | async-start | bytes 2097152 | tf_op jit(solution)/shard_map/all_to_all | solution.py:303
  84.3 30.4 %copy-start.4 = (f32[128]{0:T(128)S(1)}, f32[128]{0:T(128)}, u32[]{:S(2)}) copy-start(f32[128]{0:T(128)} %param.12) | copy-start | bytes 1540
  84.3 1.2 %copy-start = (bf16[32,128,128]{2,1,0:T(8,128)(2,1)S(1)}, bf16[32,128,128]{2,1,0:T(8,128)(2,1)}, u32[]{:S(2)}) copy-start(bf16[32,128,128]{2,1,0:T(8,128)(2,1)} %pair_ref) | copy-start | bytes 3145732

commit v5 on v4

--- a/solution.py
+++ b/solution.py
@@ -23,13 +23,14 @@
 
 
 PARTS = 4
+STRIP = 16
 
 
 def operands_kernel(
     pair_hbm, gain_hbm, left_hbm, right_hbm, sent_ref, pair_ref, gain_ref, weights, turned, sides, arrived
 ):
     here_i, here_k, channels = pair_ref.shape
-    chips, cores, cols, _, half, _ = sent_ref.shape
+    chips, cols = sent_ref.shape[:2]
     wide = left_hbm.shape[1]
     width, part = wide // 2, here_i // PARTS
     pieces = [
@@ -50,9 +51,10 @@
     for side in range(2):
         turned[side * wide : (side + 1) * wide] = (0.5 * weights[side].astype(F32)).T.astype(BF16)
     gain = gain_ref[...]
-    for core in range(cores):
-        for i in range(0, half, 2):
-            row = core * half + i
+    for start in range(0, here_i, STRIP):
+        strip = start // STRIP
+        for i in range(0, STRIP, 2):
+            row = start + i
             if row % part == 0:
                 pieces[row // part].wait()
             rows = pair_ref[row : row + 2].reshape(2 * here_k, channels).astype(F32)
@@ -63,16 +65,18 @@
             for side in range(2):
                 one = both[side * wide : (side + 1) * wide]
                 gated = (jnp.tanh(one[:width]) + 1.0) * one[width:]
-                sides[core, side, i] = gated[:, :here_k]
-                sides[core, side, i + 1] = gated[:, here_k:]
+                sides[strip, side, i] = gated[:, :here_k]
+                sides[strip, side, i + 1] = gated[:, here_k:]
         for side in range(2):
-            by_channel = jnp.swapaxes(sides[core, side], 0, 1).astype(BF16)
-            sent_ref[:, core, :, side] = by_channel.reshape(chips, cols, half, here_k)
+            by_channel = jnp.swapaxes(sides[strip, side], 0, 1).astype(BF16)
+            sent_ref[:, :, side, start : start + STRIP] = by_channel.reshape(
+                chips, cols, STRIP, here_k
+            )
 
 
 def operands(pair, gain, proj_left, proj_right, chips, cols):
     here_i, here_k, channels = pair.shape
-    half, wide = here_i // 2, proj_left.shape[1]
+    wide = proj_left.shape[1]
     hbm = pl.BlockSpec(memory_space=pltpu.HBM)
     arrays = [
         pltpu.with_memory_space_constraint(array, pltpu.HBM)
@@ -82,13 +86,13 @@
         operands_kernel,
         in_specs=[hbm] * 4,
         out_specs=pl.BlockSpec(memory_space=pltpu.VMEM),
-        out_shape=jax.ShapeDtypeStruct((chips, 2, cols, 2, half, here_k), BF16),
+        out_shape=jax.ShapeDtypeStruct((chips, cols, 2, here_i, here_k), BF16),
         scratch_shapes=[
             pltpu.VMEM(pair.shape, BF16),
             pltpu.VMEM(gain.shape, F32),
             pltpu.VMEM((2, channels, wide), BF16),
             pltpu.VMEM((2 * wide, channels), BF16),
-            pltpu.VMEM((2, 2, half, wide // 2, here_k), F32),
+            pltpu.VMEM((here_i // STRIP, 2, STRIP, wide // 2, here_k), F32),
             pltpu.SemaphoreType.DMA((PARTS + 3,)),
         ],
         compiler_params=pltpu.CompilerParams(vmem_limit_bytes=VMEM_LIMIT),
@@ -229,29 +233,28 @@
 
 
 def update_kernel(
-    odd_ref, back_ref, gain_ref, weight_ref, gate_ref, update_hbm, update_ref, left
+    first_ref, back_ref, gain_ref, weight_ref, gate_ref, update_hbm, update_ref, left
 ):
-    chips, cores, cols, half, here_k = back_ref.shape
-    width, each = chips * cols, gate_ref.shape[1]
-    channels = gate_ref.shape[4]
-    odd = odd_ref[0]
+    chips, cols, here_i, here_k = back_ref.shape
+    width = chips * cols
+    _, each, _, run, channels = gate_ref.shape
+    first = first_ref[0]
+    second = 1 - first
     gain = jnp.broadcast_to(gain_ref[...], (here_k, width)).T
     outgoing = []
-    for c in range(cores):
-        product = back_ref[:, c].reshape(width, half, here_k).astype(F32)
+    for start in range(0, here_i, STRIP):
+        product = back_ref[:, :, start : start + STRIP].reshape(width, STRIP, here_k).astype(F32)
         average = jnp.mean(product, axis=0, keepdims=True)
         centered = product - average
         spread = jnp.mean(centered * centered, axis=0, keepdims=True)
         normed = centered * lax.rsqrt(spread + 1e-05)
         normed = (jnp.swapaxes(normed, 0, 1) * gain).astype(BF16)
-        first = (c + odd) % 2
-        for i in range(half):
-            row = c * half + i
+        for i in range(STRIP):
+            row = start + i
             projected = lax.dot_general(
                 normed[i], weight_ref[...], (((0,), (0,)), ((), ())), preferred_element_type=F32
-            ).reshape(2, each, half, channels)
+            ).reshape(2, each, run, channels)
             update_ref[row, :, first] = (gate_ref[row, :, first] * projected[0]).astype(BF16)
-            second = 1 - first
             update_ref[row, :, second] = (gate_ref[row, :, second] * projected[1]).astype(BF16)
             if (i + 1) % 4 == 0:
                 span = pl.ds(row - 3, 4)
@@ -264,10 +267,9 @@
         copy.wait()
 
 
-def updates(odd, back, gain, weight, gate):
-    chips, _, cols, half, here_k = back.shape
-    here_i, _, channels = gate.shape
-    blocked = (here_i, here_k // (2 * half), 2, half, channels)
+def updates(first, back, gain, weight, gate):
+    here_i, here_k, channels = gate.shape
+    blocked = (here_i, here_k // (2 * here_i), 2, here_i, channels)
     vmem, hbm = pl.BlockSpec(memory_space=pltpu.VMEM), pl.BlockSpec(memory_space=pltpu.HBM)
     update = pl.pallas_call(
         update_kernel,
@@ -280,37 +282,38 @@
         ],
         compiler_params=pltpu.CompilerParams(vmem_limit_bytes=VMEM_LIMIT),
         name="updates",
-    )(odd, back, gain, weight, gate.reshape(blocked))
+    )(first, back, gain, weight, gate.reshape(blocked))
     return update.reshape(gate.shape)
 
 
-def shards(rows, cols, pair, ln_in_gain, proj_left, proj_right, gate_weight, ln_out_gain, out_weight):
+def shards(chips, cols, pair, ln_in_gain, proj_left, proj_right, gate_weight, ln_out_gain, out_weight):
     width = out_weight.shape[0]
     here_i, here_k = pair.shape[0], pair.shape[1]
-    half, chips = here_i // 2, rows // 2
-    both = ("row", "col")
     exchange = functools.partial(
-        lax.all_to_all, axis_name=both, split_axis=0, concat_axis=0, tiled=True
+        lax.all_to_all, axis_name=("chip", "col"), split_axis=0, concat_axis=0, tiled=True
     )
     gain = ln_in_gain.reshape(1, -1)
     sent = operands(pair, gain, proj_left, proj_right, chips, cols)
-    got = exchange(sent.reshape(rows * cols, 2, half, here_k))
-    got = got.reshape(rows, cols, 2, half, here_k)
-    other = lax.ppermute(split(got), "row", [(r, r ^ 1) for r in range(rows)])
+    got = exchange(sent.reshape(chips * cols, 2, here_i, here_k))
+    got = got.reshape(chips, cols, 2, here_i, here_k)
+    other = lax.ppermute(split(got), "core", [(0, 1), (1, 0)])
     left, own = own_part(got)
     product = merge(left, own, other)
     product, late_pair = lax.optimization_barrier((product, pair))
-    back = exchange(product.reshape(rows * cols, half, here_k))
+    back = exchange(product.reshape(chips * cols, here_i, here_k))
     gate = gates(late_pair, gain, gate_weight)
-    odd = lax.rem(lax.axis_index("col"), 2).reshape(1)
+    first = lax.rem(lax.axis_index("core") + lax.axis_index("col"), 2).reshape(1)
     return updates(
-        odd, back.reshape(chips, 2, cols, half, here_k), ln_out_gain.reshape(1, width), out_weight, gate
+        first, back.reshape(chips, cols, here_i, here_k), ln_out_gain.reshape(1, width), out_weight, gate
     )
 
 
 def solution(mesh):
     rows, cols = mesh.shape["row"], mesh.shape["col"]
-    in_specs = (P("row", "col", None), P(), P(), P(), P(), P(), P())
-    out_specs = P("row", "col", None)
-    step = functools.partial(shards, rows, cols)
-    return jax.shard_map(step, mesh=mesh, in_specs=in_specs, out_specs=out_specs, check_vma=False)
+    chips = rows // 2
+    by_core = jax.sharding.Mesh(mesh.devices.reshape(chips, 2, cols), ("chip", "core", "col"))
+    cells = P(("chip", "core"), "col", None)
+    step = functools.partial(shards, chips, cols)
+    return jax.shard_map(
+        step, mesh=by_core, in_specs=(cells,) + (P(),) * 6, out_specs=cells, check_vma=False
+    )

time: 117 us -> 117 us (level)
  starting transfers between devices: 6.74 us -> 9.01 us
  waiting for transfers between devices: 28.9 us -> 27.3 us
  blocking collectives: 68.6 us -> 67.3 us
    ppermute x1, starting transfers between devices: 0.09 us -> 2.71 us  [shards(): other = lax.ppermute(split(got), 'core', [(0, 1), (1, 0)])]
    all_to_all x1, blocking collectives: 68.6 us -> 67.3 us  [shards(): got = exchange(sent.reshape(chips * cols, 2, here_i, here_k))]
    all_to_all x1, waiting for transfers between devices: 27.1 us -> 25.9 us  [shards(): back = exchange(product.reshape(chips * cols, here_i, here_k))]
where the time goes in v5:
time: 117 us; the launch traced here: 116 us
  blocking collectives  67.3 us (58%)
  waiting for transfers between devices  27.3 us (23%)
  Pallas kernels  11.4 us (10%)
  starting transfers between devices  9.01 us (8%)
  local copies, waits for them, and re-layouts  1.24 us (1%)
    all_to_all x1, blocking collectives, shards(): got = exchange(sent.reshape(chips * cols, 2, here_i, here_k))  67.3 us
    all_to_all x1, waiting for transfers between devices, shards(): back = exchange(product.reshape(chips * cols, here_i, here_k))  25.9 us
    all_to_all x1, starting transfers between devices, shards(): back = exchange(product.reshape(chips * cols, here_i, here_k))  6.3 us
    pallas_call x1, Pallas kernels, operands(): pl.pallas_call(operands_kernel, in_specs=[hbm] * 4, out_specs=pl.BlockSpe...  4.39 us
    ppermute x1, starting transfers between devices, shards(): other = lax.ppermute(split(got), 'core', [(0, 1), (1, 0)])  2.71 us
    pallas_call x1, Pallas kernels, updates(): pl.pallas_call(update_kernel, in_specs=[pl.BlockSpec(memory_space=pltpu.S...  2.35 us
  transfers between devices with their start and end apart: 2, of which 2 were waited for; matrix products, arithmetic and copies ran while one was open for 0% of the time, Pallas kernels for 2%

profile of v5, /device:TPU:1, one launch (start us, length us, event | category | flops | bytes accessed | tf_op | source)
XLA Modules:
  0.0 116.3 jit_solution(5055174601542772760)
XLA Ops:
  0.0 4.4 %operands.1 = bf16[16,8,2,32,128]{4,3,2,1,0:T(8,128)(2,1)S(1)} custom-call(bf16[32,128,128]{2,1,0:T(8,128)(2,1)} %pair_ref, f32[1,128]{1,0:T(1,128)} %bitcast.14, bf16[128,256]{1,0:T(8,128)(2,1)} %left_hbm.1, bf16[128,256]{1,0:T(8,128)(2,1)} %right_hbm.1), custom_call_target="tpu_custom_call" | custom-call | tf_op jit(solution)/shard_map/operands/pallas_call | solution.py:85
  4.4 67.3 %all_to_all.10 = bf16[128,2,32,128]{3,2,1,0:T(8,128)(2,1)S(1)} all-to-all(bf16[128,2,32,128]{3,2,1,0:T(8,128)(2,1)S(1)} %bitcast.12), channel_id=1, replica_groups=mesh['chip'=16,'core'=2,'col'=8] {'chip','col'}, dimensions={0} | all-to-all | bytes 4194304 | tf_op jit(solution)/shard_map/all_to_all | solution.py:297
  71.7 0.1 split.1
  71.7 2.7 %collective-permute-start = (bf16[16,8,32,128]{3,2,1,0:T(8,128)(2,1)S(1)}, bf16[16,8,32,128]{3,2,1,0:T(8,128)(2,1)S(1)}, u32[]{:S(2)}, u32[]{:S(2)}) collective-permute-start(bf16[16,8,32,128]{3,2,1,0:T(8,128)(2,1)S(1)} %split.1), channel_id=1, source_target_pairs={{0,8},{8,0},{1,9},{9,1},{2,10},{10,2},{3,11},{11,3},{4,12},{12,4},... | collective-permute-start | bytes 3145736 | tf_op jit(solution)/shard_map/ppermute | solution.py:299
  74.4 0.8 own_part.1
  75.2 1.5 %collective-permute-done.other_ref = bf16[16,8,32,128]{3,2,1,0:T(8,128)(2,1)S(1)} collective-permute-done((bf16[16,8,32,128]{3,2,1,0:T(8,128)(2,1)S(1)}, bf16[16,8,32,128]{3,2,1,0:T(8,128)(2,1)S(1)}, u32[]{:S(2)}, u32[]{:S(2)}) %collective-permute-start) | collective-permute-done | bytes 1048608 | tf_op jit(solution)/shard_map/ppermute | solution.py:299
  76.7 0.0 copy-start.1
  76.7 0.0 copy-start.3
  76.7 1.8 %merge.1 = bf16[16,8,32,128]{3,2,1,0:T(8,128)(2,1)} custom-call(bf16[512,1024]{1,0:T(8,128)(2,1)S(1)} %get-tuple-element.9.left_ref, bf16[512,512]{1,0:T(8,128)(2,1)S(1)} %get-tuple-element.10.own_ref, bf16[16,8,32,128]{3,2,1,0:T(8,128)(2,1)S(1)} %collective-permute-done.other_ref), custom_call_target="tpu_custom_call" | custom-call | tf_op jit(solution)/shard_map/merge/pallas_call | solution.py:190
  78.5 0.0 copy-start.2
  78.5 6.3 %all-to-all-start.1 = ((bf16[128,32,128]{2,1,0:T(8,128)(2,1)}), bf16[128,32,128]{2,1,0:T(8,128)(2,1)S(1)}, u32[]{:S(2)}, u32[]{:S(2)}) async-start(bf16[128,32,128]{2,1,0:T(8,128)(2,1)} %bitcast.4), calls=%async_computation.1 | async-start | bytes 2097152 | tf_op jit(solution)/shard_map/all_to_all | solution.py:303
  84.9 0.0 copy-start.4
  84.9 0.0 copy-done.1
  84.9 0.0 copy-done.3
  84.9 0.0 copy-start
  84.9 1.2 %copy-done = bf16[32,128,128]{2,1,0:T(8,128)(2,1)S(1)} copy-done((bf16[32,128,128]{2,1,0:T(8,128)(2,1)S(1)}, bf16[32,128,128]{2,1,0:T(8,128)(2,1)}, u32[]{:S(2)}) %copy-start) | copy-done | bytes 1048600
  86.1 2.0 %gates.1 = f32[32,128,128]{2,1,0:T(8,128)S(1)} custom-call(bf16[32,128,128]{2,1,0:T(8,128)(2,1)S(1)} %copy-done, f32[1,128]{1,0:T(1,128)S(1)} %bitcast.15, bf16[128,128]{1,0:T(8,128)(2,1)S(1)} %copy-done.1), custom_call_target="tpu_custom_call" | custom-call | flops 134217728 | bytes 3145728 | tf_op jit(solution)/shard_map/gates/pallas_call | solution.py:217
  88.1 25.9 %all-to-all-done.1 = bf16[128,32,128]{2,1,0:T(8,128)(2,1)S(1)} async-done(((bf16[128,32,128]{2,1,0:T(8,128)(2,1)}), bf16[128,32,128]{2,1,0:T(8,128)(2,1)S(1)}, u32[]{:S(2)}, u32[]{:S(2)}) %all-to-all-start.1) | async-done | bytes 1048608 | tf_op jit(solution)/shard_map/all_to_all | solution.py:303
  114.0 0.0 copy-done.2
  114.0 0.0 copy-done.4
  114.0 2.4 %updates.1 = bf16[32,2,2,32,128]{4,3,2,1,0:T(8,128)(2,1)} custom-call(s32[1]{0:T(128)} %bitcast.first_ref, bf16[16,8,32,128]{3,2,1,0:T(8,128)(2,1)S(1)} %bitcast.13, f32[1,128]{1,0:T(1,128)S(1)} %bitcast.16, bf16[128,128]{1,0:T(8,128)(2,1)S(1)} %copy-done.2, f32[32,2,2,32,128]{4,3,2,1,0:T(8,128)S(1)} %bitcast.11), custom_call_target="tpu_custom_call" | custom-call | tf_op jit(solution)/shard_map/updates/pallas_call | solution.py:274
Async XLA Ops:
  71.7 5.0 %collective-permute-start = (bf16[16,8,32,128]{3,2,1,0:T(8,128)(2,1)S(1)}, bf16[16,8,32,128]{3,2,1,0:T(8,128)(2,1)S(1)}, u32[]{:S(2)}, u32[]{:S(2)}) collective-permute-start(bf16[16,8,32,128]{3,2,1,0:T(8,128)(2,1)S(1)} %split.1), channel_id=1, source_target_pairs={{0,8},{8,0},{1,9},{9,1},{2,10},{10,2},{3,11},{11,3},{4,12},{12,4},... | collective-permute-start | bytes 3145736 | tf_op jit(solution)/shard_map/ppermute | solution.py:299
  76.7 8.2 %copy-start.1 = (bf16[128,128]{1,0:T(8,128)(2,1)S(1)}, bf16[128,128]{1,0:T(8,128)(2,1)}, u32[]{:S(2)}) copy-start(bf16[128,128]{1,0:T(8,128)(2,1)} %weight_ref.2) | copy-start | bytes 98308
  76.7 8.2 %copy-start.3 = (f32[128]{0:T(128)S(1)}, f32[128]{0:T(128)}, u32[]{:S(2)}) copy-start(f32[128]{0:T(128)} %param.8) | copy-start | bytes 1540
  78.5 35.4 %copy-start.2 = (bf16[128,128]{1,0:T(8,128)(2,1)S(1)}, bf16[128,128]{1,0:T(8,128)(2,1)}, u32[]{:S(2)}) copy-start(bf16[128,128]{1,0:T(8,128)(2,1)} %weight_ref.3) | copy-start | bytes 98308
  78.5 35.4 %all-to-all-start.1 = ((bf16[128,32,128]{2,1,0:T(8,128)(2,1)}), bf16[128,32,128]{2,1,0:T(8,128)(2,1)S(1)}, u32[]{:S(2)}, u32[]{:S(2)}) async-start(bf16[128,32,128]{2,1,0:T(8,128)(2,1)} %bitcast.4), calls=%async_computation.1 | async-start | bytes 2097152 | tf_op jit(solution)/shard_map/all_to_all | solution.py:303
  84.9 29.1 %copy-start.4 = (f32[128]{0:T(128)S(1)}, f32[128]{0:T(128)}, u32[]{:S(2)}) copy-start(f32[128]{0:T(128)} %param.12) | copy-start | bytes 1540
  84.9 1.2 %copy-start = (bf16[32,128,128]{2,1,0:T(8,128)(2,1)S(1)}, bf16[32,128,128]{2,1,0:T(8,128)(2,1)}, u32[]{:S(2)}) copy-start(bf16[32,128,128]{2,1,0:T(8,128)(2,1)} %pair_ref) | copy-start | bytes 3145732

commit v6 on v5

--- a/solution.py
+++ b/solution.py
@@ -9,10 +9,6 @@
 
 F32, BF16 = jnp.float32, jnp.bfloat16
 VMEM_LIMIT = 40 * 1024 * 1024
-
-
-def sigmoid(values):
-    return 0.5 * jnp.tanh(0.5 * values) + 0.5
 
 
 def normalize(values, gain):
@@ -117,7 +113,18 @@
     )(got)
 
 
-def own_kernel(got_ref, left_ref, own_ref, right):
+def own_kernel(
+    got_ref, pair_hbm, gain_hbm, weight_hbm, left_ref, own_ref, gate_ref,
+    right, pair_ref, gain_ref, weight_ref, arrived,
+):
+    incoming = [
+        pltpu.make_async_copy(source, target, arrived.at[n])
+        for n, (source, target) in enumerate(
+            ((weight_hbm, weight_ref), (gain_hbm, gain_ref), (pair_hbm, pair_ref))
+        )
+    ]
+    for copy in incoming:
+        copy.start()
     rows, cols, _, half, here_k = got_ref.shape
     for s in range(cols):
         span = pl.ds(s * here_k, here_k)
@@ -128,30 +135,48 @@
         own_ref[:, j : j + step] = lax.dot_general(
             left_ref[...], right[j : j + step], (((1,), (1,)), ((), ())), preferred_element_type=F32
         ).astype(BF16)
-
-
-def own_part(got):
+    for copy in incoming:
+        copy.wait()
+    weight = (0.5 * weight_ref[...].astype(F32)).astype(BF16)
+    here_i, _, channels = pair_ref.shape
+    for i in range(0, here_i, 4):
+        some = pair_ref[i : i + 4].reshape(4 * here_k, channels).astype(F32)
+        gate = jnp.dot(normalize(some, gain_ref[...]), weight, preferred_element_type=F32)
+        gate_ref[i : i + 4] = (jnp.tanh(gate) + 1.0).reshape(4, here_k, channels)
+
+
+def own_part(got, pair, gain, gate_weight):
     rows, cols, _, half, here_k = got.shape
     tall, deep = rows * half, cols * here_k
-    vmem = pl.BlockSpec(memory_space=pltpu.VMEM)
+    vmem, hbm = pl.BlockSpec(memory_space=pltpu.VMEM), pl.BlockSpec(memory_space=pltpu.HBM)
+    arrays = [
+        pltpu.with_memory_space_constraint(array, pltpu.HBM) for array in (pair, gain, gate_weight)
+    ]
     return pl.pallas_call(
         own_kernel,
-        in_specs=[vmem],
-        out_specs=[vmem, vmem],
+        in_specs=[vmem, hbm, hbm, hbm],
+        out_specs=[vmem, vmem, vmem],
         out_shape=[
             jax.ShapeDtypeStruct((tall, deep), BF16),
             jax.ShapeDtypeStruct((tall, tall), BF16),
-        ],
-        scratch_shapes=[pltpu.VMEM((tall, deep), BF16)],
+            jax.ShapeDtypeStruct(pair.shape, F32),
+        ],
+        scratch_shapes=[
+            pltpu.VMEM((tall, deep), BF16),
+            pltpu.VMEM(pair.shape, BF16),
+            pltpu.VMEM(gain.shape, F32),
+            pltpu.VMEM(gate_weight.shape, BF16),
+            pltpu.SemaphoreType.DMA((3,)),
+        ],
         compiler_params=pltpu.CompilerParams(vmem_limit_bytes=VMEM_LIMIT),
         cost_estimate=pl.CostEstimate(
-            flops=2 * tall * tall * deep, bytes_accessed=8 * tall * deep, transcendentals=0
+            flops=2 * tall * tall * deep, bytes_accessed=8 * tall * deep, transcendentals=pair.size
         ),
         name="own_part",
-    )(got)
-
-
-def merge_kernel(left_ref, own_ref, other_ref, product_hbm, product_ref, right, left):
+    )(got, *arrays)
+
+
+def merge_kernel(left_ref, own_ref, other_ref, product_ref, right):
     rows, cols, half, here_k = other_ref.shape
     each = rows // cols * half
     for s in range(cols):
@@ -159,7 +184,6 @@
         block = other_ref[:, s].reshape(cols // 2, 2, each, here_k)
         right[:, 1, :, span] = block[:, 0]
         right[:, 0, :, span] = block[:, 1]
-    outgoing = []
     first = lax.broadcasted_iota(jnp.int32, (1, here_k), 1) < each
     for pair in range(0, cols // 2, 2):
         part = right[pair : pair + 2].reshape(2 * here_k, cols * here_k)
@@ -174,14 +198,6 @@
             odd = jnp.where(first, other, own).astype(BF16)
             product_ref[:, 2 * (pair + p)] = even.reshape(rows, half, here_k)
             product_ref[:, 2 * (pair + p) + 1] = odd.reshape(rows, half, here_k)
-            span = pl.ds(2 * (pair + p), 2)
-            copy = pltpu.make_async_copy(
-                product_ref.at[:, span], product_hbm.at[:, span], left.at[pair + p]
-            )
-            copy.start()
-            outgoing.append(copy)
-    for copy in outgoing:
-        copy.wait()
 
 
 def merge(left, own, other):
@@ -190,57 +206,31 @@
     return pl.pallas_call(
         merge_kernel,
         in_specs=[vmem, vmem, vmem],
-        out_specs=pl.BlockSpec(memory_space=pltpu.HBM),
+        out_specs=vmem,
         out_shape=jax.ShapeDtypeStruct(other.shape, BF16),
         scratch_shapes=[
-            pltpu.VMEM(other.shape, BF16),
             pltpu.VMEM((cols // 2, 2, rows // cols * half, cols * here_k), BF16),
-            pltpu.SemaphoreType.DMA((cols // 2,)),
         ],
         compiler_params=pltpu.CompilerParams(vmem_limit_bytes=VMEM_LIMIT),
         name="merge",
     )(left, own, other)
 
 
-def gate_kernel(pair_ref, gain_ref, weight_ref, gate_ref):
-    some, here_k, channels = pair_ref.shape
-    rows = pair_ref[...].reshape(some * here_k, channels).astype(F32)
-    normed = normalize(rows, gain_ref[...])
-    gate = sigmoid(jnp.dot(normed, weight_ref[...], preferred_element_type=F32))
-    gate_ref[...] = gate.reshape(gate_ref.shape)
-
-
-def gates(pair, gain, weight):
-    here_i, here_k, channels = pair.shape
-    some = here_i // 4
-    block = pl.BlockSpec((some, here_k, channels), lambda i: (i, 0, 0))
-    return pl.pallas_call(
-        gate_kernel,
-        grid=(4,),
-        in_specs=[
-            block,
-            pl.BlockSpec(gain.shape, lambda i: (0, 0)),
-            pl.BlockSpec(weight.shape, lambda i: (0, 0)),
-        ],
-        out_specs=block,
-        out_shape=jax.ShapeDtypeStruct(pair.shape, F32),
-        compiler_params=pltpu.CompilerParams(vmem_limit_bytes=VMEM_LIMIT),
-        cost_estimate=pl.CostEstimate(
-            flops=2 * pair.size * channels, bytes_accessed=6 * pair.size, transcendentals=pair.size
-        ),
-        name="gates",
-    )(pair, gain, weight)
-
-
 def update_kernel(
-    first_ref, back_ref, gain_ref, weight_ref, gate_ref, update_hbm, update_ref, left
+    first_ref, back_ref, gain_hbm, weight_hbm, gate_ref, update_hbm,
+    gain_ref, weight_ref, update_ref, arrived, left,
 ):
     chips, cols, here_i, here_k = back_ref.shape
     width = chips * cols
     _, each, _, run, channels = gate_ref.shape
     first = first_ref[0]
     second = 1 - first
-    gain = jnp.broadcast_to(gain_ref[...], (here_k, width)).T
+    incoming = [
+        pltpu.make_async_copy(gain_hbm, gain_ref, arrived.at[0]),
+        pltpu.make_async_copy(weight_hbm, weight_ref, arrived.at[1]),
+    ]
+    for copy in incoming:
+        copy.start()
     outgoing = []
     for start in range(0, here_i, STRIP):
         product = back_ref[:, :, start : start + STRIP].reshape(width, STRIP, here_k).astype(F32)
@@ -248,11 +238,16 @@
         centered = product - average
         spread = jnp.mean(centered * centered, axis=0, keepdims=True)
         normed = centered * lax.rsqrt(spread + 1e-05)
+        if start == 0:
+            for copy in incoming:
+                copy.wait()
+            gain = jnp.broadcast_to(gain_ref[...], (here_k, width)).T
+            weight = (0.5 * weight_ref[...].astype(F32)).astype(BF16)
         normed = (jnp.swapaxes(normed, 0, 1) * gain).astype(BF16)
         for i in range(STRIP):
             row = start + i
             projected = lax.dot_general(
-                normed[i], weight_ref[...], (((0,), (0,)), ((), ())), preferred_element_type=F32
+                normed[i], weight, (((0,), (0,)), ((), ())), preferred_element_type=F32
             ).reshape(2, each, run, channels)
             update_ref[row, :, first] = (gate_ref[row, :, first] * projected[0]).astype(BF16)
             update_ref[row, :, second] = (gate_ref[row, :, second] * projected[1]).astype(BF16)
@@ -271,13 +266,17 @@
     here_i, here_k, channels = gate.shape
     blocked = (here_i, here_k // (2 * here_i), 2, here_i, channels)
     vmem, hbm = pl.BlockSpec(memory_space=pltpu.VMEM), pl.BlockSpec(memory_space=pltpu.HBM)
+    gain, weight = (pltpu.with_memory_space_constraint(array, pltpu.HBM) for array in (gain, weight))
     update = pl.pallas_call(
         update_kernel,
-        in_specs=[pl.BlockSpec(memory_space=pltpu.SMEM), vmem, vmem, vmem, vmem],
+        in_specs=[pl.BlockSpec(memory_space=pltpu.SMEM), vmem, hbm, hbm, vmem],
         out_specs=hbm,
         out_shape=jax.ShapeDtypeStruct(blocked, BF16),
         scratch_shapes=[
+            pltpu.VMEM(gain.shape, F32),
+            pltpu.VMEM(weight.shape, BF16),
             pltpu.VMEM(blocked, BF16),
+            pltpu.SemaphoreType.DMA((2,)),
             pltpu.SemaphoreType.DMA((here_i // 4,)),
         ],
         compiler_params=pltpu.CompilerParams(vmem_limit_bytes=VMEM_LIMIT),
@@ -297,12 +296,11 @@
     got = exchange(sent.reshape(chips * cols, 2, here_i, here_k))
     got = got.reshape(chips, cols, 2, here_i, here_k)
     other = lax.ppermute(split(got), "core", [(0, 1), (1, 0)])
-    left, own = own_part(got)
+    left, own, gate = own_part(got, pair, gain, gate_weight)
     product = merge(left, own, other)
-    product, late_pair = lax.optimization_barrier((product, pair))
+    first = lax.rem(lax.axis_index("core") + lax.axis_index("col"), 2).reshape(1)
+    product, first = lax.optimization_barrier((product, first))
     back = exchange(product.reshape(chips * cols, here_i, here_k))
-    gate = gates(late_pair, gain, gate_weight)
-    first = lax.rem(lax.axis_index("core") + lax.axis_index("col"), 2).reshape(1)
     return updates(
         first, back.reshape(chips, cols, here_i, here_k), ln_out_gain.reshape(1, width), out_weight, gate
     )

time: 117 us -> 118 us (level)
  blocking collectives: 67.3 us -> 103 us
  waiting for transfers between devices: 27.3 us -> 0.01 us
  starting transfers between devices: 9.01 us -> 2.62 us
  local copies, waits for them, and re-layouts: 1.24 us -> 0 us
    all_to_all x0 -> x1, blocking collectives: none -> 35.5 us  [shards(): back = exchange(product.reshape(chips * cols, here_i, here_k))]
    all_to_all x1 -> x0, waiting for transfers between devices: 25.9 us -> none  [shards(): back = exchange(product.reshape(chips * cols, here_i, here_k))]
    all_to_all x1 -> x0, starting transfers between devices: 6.3 us -> none  [shards(): back = exchange(product.reshape(chips * cols, here_i, here_k))]
    ppermute x1, waiting for transfers between devices: 1.47 us -> 0.01 us  [shards(): other = lax.ppermute(split(got), 'core', [(0, 1), (1, 0)])]
    unnamed x10 -> x0, local copies, waits for them, and re-layouts: 1.24 us -> none
    pallas_call x3 -> x2, Pallas kernels: 4.58 us -> 3.74 us  [the longest x1 2.94 us: own_part(): pl.pallas_call(own_kernel, in_specs=[vmem, hbm, hbm, hbm], out_specs=[vme...]
  transfers between devices with their start and end apart: 2 -> 1, of which waited for: 2 -> 0; matrix products, arithmetic and copies ran while one was open for 0% -> 0% of each run, Pallas kernels for 2% -> 3%
where the time goes in v6:
time: 118 us; the launch traced here: 117 us
  blocking collectives  103 us (87%)
  Pallas kernels  12 us (10%)
  starting transfers between devices  2.62 us (2%)
    all_to_all x1, blocking collectives, shards(): got = exchange(sent.reshape(chips * cols, 2, here_i, here_k))  67.3 us
    all_to_all x1, blocking collectives, shards(): back = exchange(product.reshape(chips * cols, here_i, here_k))  35.5 us
    pallas_call x1, Pallas kernels, operands(): pl.pallas_call(operands_kernel, in_specs=[hbm] * 4, out_specs=pl.BlockSpe...  4.39 us
    pallas_call x1, Pallas kernels, own_part(): pl.pallas_call(own_kernel, in_specs=[vmem, hbm, hbm, hbm], out_specs=[vme...  2.94 us
    pallas_call x1, Pallas kernels, updates(): pl.pallas_call(update_kernel, in_specs=[pl.BlockSpec(memory_space=pltpu.S...  2.86 us
    ppermute x1, starting transfers between devices, shards(): other = lax.ppermute(split(got), 'core', [(0, 1), (1, 0)])  2.62 us
  transfers between devices with their start and end apart: 1, of which 0 were waited for; matrix products, arithmetic and copies ran while one was open for 0% of the time, Pallas kernels for 3%

profile of v6, /device:TPU:1, one launch (start us, length us, event | category | flops | bytes accessed | tf_op | source)
XLA Modules:
  0.0 117.5 jit_solution(4964091474308355864)
XLA Ops:
  0.0 4.4 %operands.1 = bf16[16,8,2,32,128]{4,3,2,1,0:T(8,128)(2,1)S(1)} custom-call(bf16[32,128,128]{2,1,0:T(8,128)(2,1)} %pair_hbm.3, f32[1,128]{1,0:T(1,128)} %bitcast.15, bf16[128,256]{1,0:T(8,128)(2,1)} %left_hbm.1, bf16[128,256]{1,0:T(8,128)(2,1)} %right_hbm.1), custom_call_target="tpu_custom_call" | custom-call | tf_op jit(solution)/shard_map/operands/pallas_call | solution.py:81
  4.4 67.3 %all_to_all.10 = bf16[128,2,32,128]{3,2,1,0:T(8,128)(2,1)S(1)} all-to-all(bf16[128,2,32,128]{3,2,1,0:T(8,128)(2,1)S(1)} %bitcast.11), channel_id=1, replica_groups=mesh['chip'=16,'core'=2,'col'=8] {'chip','col'}, dimensions={0} | all-to-all | bytes 4194304 | tf_op jit(solution)/shard_map/all_to_all | solution.py:296
  71.7 1.0 split.1
  72.7 2.6 %collective-permute-start = (bf16[16,8,32,128]{3,2,1,0:T(8,128)(2,1)}, bf16[16,8,32,128]{3,2,1,0:T(8,128)(2,1)S(1)}, u32[]{:S(2)}, u32[]{:S(2)}) collective-permute-start(bf16[16,8,32,128]{3,2,1,0:T(8,128)(2,1)} %split.1), channel_id=1, source_target_pairs={{0,8},{8,0},{1,9},{9,1},{2,10},{10,2},{3,11},{11,3},{4,12},{12,4},... | collective-permute-start | bytes 3145736 | tf_op jit(solution)/shard_map/ppermute | solution.py:298
  75.3 2.9 %own_part.1 = (bf16[512,1024]{1,0:T(8,128)(2,1)S(1)}, bf16[512,512]{1,0:T(8,128)(2,1)S(1)}, f32[32,128,128]{2,1,0:T(8,128)S(1)}) custom-call(bf16[16,8,2,32,128]{4,3,2,1,0:T(8,128)(2,1)S(1)} %bitcast.10, bf16[32,128,128]{2,1,0:T(8,128)(2,1)} %pair_hbm.3, f32[1,128]{1,0:T(1,128)} %bitcast.16, bf16[128,128]{1,0:T(8,128)(2,1)} %weight_hbm.2), custom_call_target="tpu_custom_call" | custom-call | flops 536870912 | bytes 4194304 | tf_op jit(solution)/shard_map/own_part/pallas_call | solution.py:155
  78.3 0.0 collective-permute-done.other_ref
  78.3 0.8 merge.1
  79.1 35.5 %all_to_all.11 = bf16[128,32,128]{2,1,0:T(8,128)(2,1)S(1)} all-to-all(bf16[128,32,128]{2,1,0:T(8,128)(2,1)S(1)} %bitcast.13), channel_id=1, replica_groups=mesh['chip'=16,'core'=2,'col'=8] {'chip','col'}, dimensions={0} | all-to-all | bytes 2097152 | tf_op jit(solution)/shard_map/all_to_all | solution.py:303
  114.6 2.9 %updates.1 = bf16[32,2,2,32,128]{4,3,2,1,0:T(8,128)(2,1)} custom-call(s32[1]{0:T(128)} %bitcast.3.first_ref, bf16[16,8,32,128]{3,2,1,0:T(8,128)(2,1)S(1)} %bitcast.12, f32[1,128]{1,0:T(1,128)} %bitcast.17, bf16[128,128]{1,0:T(8,128)(2,1)} %weight_hbm.3, f32[32,2,2,32,128]{4,3,2,1,0:T(8,128)S(1)} %bitcast.14), custom_call_target="tpu_custom_call" | custom-call | tf_op jit(solution)/shard_map/updates/pallas_call | solution.py:270
Async XLA Ops:
  72.7 5.6 %collective-permute-start = (bf16[16,8,32,128]{3,2,1,0:T(8,128)(2,1)}, bf16[16,8,32,128]{3,2,1,0:T(8,128)(2,1)S(1)}, u32[]{:S(2)}, u32[]{:S(2)}) collective-permute-start(bf16[16,8,32,128]{3,2,1,0:T(8,128)(2,1)} %split.1), channel_id=1, source_target_pairs={{0,8},{8,0},{1,9},{9,1},{2,10},{10,2},{3,11},{11,3},{4,12},{12,4},... | collective-permute-start | bytes 3145736 | tf_op jit(solution)/shard_map/ppermute | solution.py:298

commit v7 on v5

--- a/solution.py
+++ b/solution.py
@@ -27,7 +27,8 @@
 
 
 def operands_kernel(
-    pair_hbm, gain_hbm, left_hbm, right_hbm, sent_ref, pair_ref, gain_ref, weights, turned, sides, arrived
+    pair_hbm, gain_hbm, left_hbm, right_hbm, sent_hbm,
+    sent_ref, pair_ref, gain_ref, weights, turned, sides, arrived, left,
 ):
     here_i, here_k, channels = pair_ref.shape
     chips, cols = sent_ref.shape[:2]
@@ -51,6 +52,7 @@
     for side in range(2):
         turned[side * wide : (side + 1) * wide] = (0.5 * weights[side].astype(F32)).T.astype(BF16)
     gain = gain_ref[...]
+    outgoing = []
     for start in range(0, here_i, STRIP):
         strip = start // STRIP
         for i in range(0, STRIP, 2):
@@ -72,6 +74,14 @@
             sent_ref[:, :, side, start : start + STRIP] = by_channel.reshape(
                 chips, cols, STRIP, here_k
             )
+            span = pl.ds(start, STRIP)
+            copy = pltpu.make_async_copy(
+                sent_ref.at[:, :, side, span], sent_hbm.at[:, :, side, span], left.at[len(outgoing)]
+            )
+            copy.start()
+            outgoing.append(copy)
+    for copy in outgoing:
+        copy.wait()
 
 
 def operands(pair, gain, proj_left, proj_right, chips, cols):
@@ -85,15 +95,17 @@
     return pl.pallas_call(
         operands_kernel,
         in_specs=[hbm] * 4,
-        out_specs=pl.BlockSpec(memory_space=pltpu.VMEM),
-        out_shape=jax.ShapeDtypeStruct((chips, cols, 2, here_i, here_k), BF16),
+        out_specs=hbm,
+        out_shape=pltpu.HBM((chips, cols, 2, here_i, here_k), BF16),
         scratch_shapes=[
+            pltpu.VMEM((chips, cols, 2, here_i, here_k), BF16),
             pltpu.VMEM(pair.shape, BF16),
             pltpu.VMEM(gain.shape, F32),
             pltpu.VMEM((2, channels, wide), BF16),
             pltpu.VMEM((2 * wide, channels), BF16),
             pltpu.VMEM((here_i // STRIP, 2, STRIP, wide // 2, here_k), F32),
             pltpu.SemaphoreType.DMA((PARTS + 3,)),
+            pltpu.SemaphoreType.DMA((2 * here_i // STRIP,)),
         ],
         compiler_params=pltpu.CompilerParams(vmem_limit_bytes=VMEM_LIMIT),
         name="operands",
@@ -191,7 +203,7 @@
         merge_kernel,
         in_specs=[vmem, vmem, vmem],
         out_specs=pl.BlockSpec(memory_space=pltpu.HBM),
-        out_shape=jax.ShapeDtypeStruct(other.shape, BF16),
+        out_shape=pltpu.HBM(other.shape, BF16),
         scratch_shapes=[
             pltpu.VMEM(other.shape, BF16),
             pltpu.VMEM((cols // 2, 2, rows // cols * half, cols * here_k), BF16),
@@ -294,14 +306,15 @@
     )
     gain = ln_in_gain.reshape(1, -1)
     sent = operands(pair, gain, proj_left, proj_right, chips, cols)
+    sent, late_pair = lax.optimization_barrier((sent, pair))
     got = exchange(sent.reshape(chips * cols, 2, here_i, here_k))
+    gate = gates(late_pair, gain, gate_weight)
+    got, gate = lax.optimization_barrier((got, gate))
     got = got.reshape(chips, cols, 2, here_i, here_k)
     other = lax.ppermute(split(got), "core", [(0, 1), (1, 0)])
     left, own = own_part(got)
     product = merge(left, own, other)
-    product, late_pair = lax.optimization_barrier((product, pair))
     back = exchange(product.reshape(chips * cols, here_i, here_k))
-    gate = gates(late_pair, gain, gate_weight)
     first = lax.rem(lax.axis_index("core") + lax.axis_index("col"), 2).reshape(1)
     return updates(
         first, back.reshape(chips, cols, here_i, here_k), ln_out_gain.reshape(1, width), out_weight, gate

time: 117 us -> 119 us (1.017)
  blocking collectives: 67.3 us -> 0 us
  waiting for transfers between devices: 27.3 us -> 78.4 us
  starting transfers between devices: 9.01 us -> 25.5 us
    all_to_all x1 -> x0, blocking collectives: 67.3 us -> none  [shards(): got = exchange(sent.reshape(chips * cols, 2, here_i, here_k))]
    all_to_all x0 -> x1, waiting for transfers between devices: none -> 47.8 us  [shards(): got = exchange(sent.reshape(chips * cols, 2, here_i, here_k))]
    all_to_all x0 -> x1, starting transfers between devices: none -> 16.5 us  [shards(): got = exchange(sent.reshape(chips * cols, 2, here_i, here_k))]
    all_to_all x1, waiting for transfers between devices: 25.9 us -> 29.1 us  [shards(): back = exchange(product.reshape(chips * cols, here_i, here_k))]
  transfers between devices with their start and end apart: 2 -> 3, of which waited for: 2 -> 3; matrix products, arithmetic and copies ran while one was open for 0% -> 0% of each run, Pallas kernels for 2% -> 2%
where the time goes in v7:
time: 119 us; the launch traced here: 118 us
  waiting for transfers between devices  78.4 us (66%)
  starting transfers between devices  25.5 us (21%)
  Pallas kernels  12.3 us (10%)
  local copies, waits for them, and re-layouts  1.35 us (1%)
    all_to_all x1, waiting for transfers between devices, shards(): got = exchange(sent.reshape(chips * cols, 2, here_i, here_k))  47.8 us
    all_to_all x1, waiting for transfers between devices, shards(): back = exchange(product.reshape(chips * cols, here_i, here_k))  29.1 us
    all_to_all x1, starting transfers between devices, shards(): got = exchange(sent.reshape(chips * cols, 2, here_i, here_k))  16.5 us
    all_to_all x1, starting transfers between devices, shards(): back = exchange(product.reshape(chips * cols, here_i, here_k))  6.31 us
    pallas_call x1, Pallas kernels, operands(): pl.pallas_call(operands_kernel, in_specs=[hbm] * 4, out_specs=hbm, out_sh...  5.25 us
    ppermute x1, starting transfers between devices, shards(): other = lax.ppermute(split(got), 'core', [(0, 1), (1, 0)])  2.7 us
  transfers between devices with their start and end apart: 3, of which 3 were waited for; matrix products, arithmetic and copies ran while one was open for 0% of the time, Pallas kernels for 2%

profile of v7, /device:TPU:1, one launch (start us, length us, event | category | flops | bytes accessed | tf_op | source)
XLA Modules:
  0.0 117.6 jit_solution(10730692555946000890)
XLA Ops:
  0.0 5.2 %operands.1 = bf16[16,8,2,32,128]{4,3,2,1,0:T(8,128)(2,1)} custom-call(bf16[32,128,128]{2,1,0:T(8,128)(2,1)} %pair_ref, f32[1,128]{1,0:T(1,128)} %bitcast.13, bf16[128,256]{1,0:T(8,128)(2,1)} %left_hbm.1, bf16[128,256]{1,0:T(8,128)(2,1)} %right_hbm.1), custom_call_target="tpu_custom_call" | custom-call | tf_op jit(solution)/shard_map/operands/pallas_call | solution.py:95
  5.3 0.0 copy-start.2
  5.3 0.0 copy-start.3
  5.3 0.0 copy-start.5
  5.3 16.5 %all-to-all-start = ((bf16[128,2,32,128]{3,2,1,0:T(8,128)(2,1)}), bf16[128,2,32,128]{3,2,1,0:T(8,128)(2,1)S(1)}, u32[]{:S(2)}, u32[]{:S(2)}) async-start(bf16[128,2,32,128]{3,2,1,0:T(8,128)(2,1)} %bitcast.16), calls=%async_computation | async-start | bytes 4194304 | tf_op jit(solution)/shard_map/all_to_all | solution.py:310
  21.8 0.0 copy-done.2
  21.8 0.0 copy-done.3
  21.8 0.0 copy-done.5
  21.8 2.0 %gates.1 = f32[32,128,128]{2,1,0:T(8,128)S(1)} custom-call(bf16[32,128,128]{2,1,0:T(8,128)(2,1)S(1)} %copy-done.2, f32[1,128]{1,0:T(1,128)S(1)} %bitcast.14, bf16[128,128]{1,0:T(8,128)(2,1)S(1)} %copy-done.3), custom_call_target="tpu_custom_call" | custom-call | flops 134217728 | bytes 3145728 | tf_op jit(solution)/shard_map/gates/pallas_call | solution.py:229
  23.8 0.0 copy-start
  23.8 1.3 %copy-done = f32[32,128,128]{2,1,0:T(8,128)} copy-done((f32[32,128,128]{2,1,0:T(8,128)}, f32[32,128,128]{2,1,0:T(8,128)S(1)}, u32[]{:S(2)}) %copy-start) | copy-done | bytes 2097176
  25.1 47.8 %all-to-all-done = bf16[128,2,32,128]{3,2,1,0:T(8,128)(2,1)S(1)} async-done(((bf16[128,2,32,128]{3,2,1,0:T(8,128)(2,1)}), bf16[128,2,32,128]{3,2,1,0:T(8,128)(2,1)S(1)}, u32[]{:S(2)}, u32[]{:S(2)}) %all-to-all-start) | async-done | bytes 2097184 | tf_op jit(solution)/shard_map/all_to_all | solution.py:310
  72.9 0.1 split.1
  73.0 2.7 %collective-permute-start = (bf16[16,8,32,128]{3,2,1,0:T(8,128)(2,1)S(1)}, bf16[16,8,32,128]{3,2,1,0:T(8,128)(2,1)S(1)}, u32[]{:S(2)}, u32[]{:S(2)}) collective-permute-start(bf16[16,8,32,128]{3,2,1,0:T(8,128)(2,1)S(1)} %split.1), channel_id=1, source_target_pairs={{0,8},{8,0},{1,9},{9,1},{2,10},{10,2},{3,11},{11,3},{4,12},{12,4},... | collective-permute-start | bytes 3145736 | tf_op jit(solution)/shard_map/ppermute | solution.py:314
  75.7 0.8 own_part.1
  76.5 1.5 %collective-permute-done.other_ref = bf16[16,8,32,128]{3,2,1,0:T(8,128)(2,1)S(1)} collective-permute-done((bf16[16,8,32,128]{3,2,1,0:T(8,128)(2,1)S(1)}, bf16[16,8,32,128]{3,2,1,0:T(8,128)(2,1)S(1)}, u32[]{:S(2)}, u32[]{:S(2)}) %collective-permute-start) | collective-permute-done | bytes 1048608 | tf_op jit(solution)/shard_map/ppermute | solution.py:314
  78.0 0.0 copy-start.1
  78.0 0.0 copy-start.4
  78.0 0.0 copy-start.6
  78.0 1.8 %merge.1 = bf16[16,8,32,128]{3,2,1,0:T(8,128)(2,1)} custom-call(bf16[512,1024]{1,0:T(8,128)(2,1)S(1)} %get-tuple-element.14.left_ref, bf16[512,512]{1,0:T(8,128)(2,1)S(1)} %get-tuple-element.15.own_ref, bf16[16,8,32,128]{3,2,1,0:T(8,128)(2,1)S(1)} %collective-permute-done.other_ref), custom_call_target="tpu_custom_call" | custom-call | tf_op jit(solution)/shard_map/merge/pallas_call | solution.py:202
  79.8 6.3 %all-to-all-start.1 = ((bf16[128,32,128]{2,1,0:T(8,128)(2,1)}), bf16[128,32,128]{2,1,0:T(8,128)(2,1)S(1)}, u32[]{:S(2)}, u32[]{:S(2)}) async-start(bf16[128,32,128]{2,1,0:T(8,128)(2,1)} %bitcast.17), calls=%async_computation.1 | async-start | bytes 2097152 | tf_op jit(solution)/shard_map/all_to_all | solution.py:317
  86.1 29.1 %all-to-all-done.1 = bf16[128,32,128]{2,1,0:T(8,128)(2,1)S(1)} async-done(((bf16[128,32,128]{2,1,0:T(8,128)(2,1)}), bf16[128,32,128]{2,1,0:T(8,128)(2,1)S(1)}, u32[]{:S(2)}, u32[]{:S(2)}) %all-to-all-start.1) | async-done | bytes 1048608 | tf_op jit(solution)/shard_map/all_to_all | solution.py:317
  115.2 0.0 copy-done.1
  115.2 0.0 copy-done.4
  115.2 0.0 copy-done.6
  115.2 2.4 %updates.1 = bf16[32,2,2,32,128]{4,3,2,1,0:T(8,128)(2,1)} custom-call(s32[1]{0:T(128)} %bitcast.first_ref, bf16[16,8,32,128]{3,2,1,0:T(8,128)(2,1)S(1)} %bitcast.12, f32[1,128]{1,0:T(1,128)S(1)} %bitcast.15, bf16[128,128]{1,0:T(8,128)(2,1)S(1)} %copy-done.4, f32[32,2,2,32,128]{4,3,2,1,0:T(8,128)S(1)} %bitcast.11), custom_call_target="tpu_custom_call" | custom-call | tf_op jit(solution)/shard_map/updates/pallas_call | solution.py:286
Async XLA Ops:
  5.3 16.5 %copy-start.2 = (bf16[32,128,128]{2,1,0:T(8,128)(2,1)S(1)}, bf16[32,128,128]{2,1,0:T(8,128)(2,1)}, u32[]{:S(2)}) copy-start(bf16[32,128,128]{2,1,0:T(8,128)(2,1)} %pair_ref) | copy-start | bytes 3145732
  5.3 16.5 %copy-start.3 = (bf16[128,128]{1,0:T(8,128)(2,1)S(1)}, bf16[128,128]{1,0:T(8,128)(2,1)}, u32[]{:S(2)}) copy-start(bf16[128,128]{1,0:T(8,128)(2,1)} %weight_ref.2) | copy-start | bytes 98308
  5.3 16.5 %copy-start.5 = (f32[128]{0:T(128)S(1)}, f32[128]{0:T(128)}, u32[]{:S(2)}) copy-start(f32[128]{0:T(128)} %param.8) | copy-start | bytes 1540
  5.3 67.6 %all-to-all-start = ((bf16[128,2,32,128]{3,2,1,0:T(8,128)(2,1)}), bf16[128,2,32,128]{3,2,1,0:T(8,128)(2,1)S(1)}, u32[]{:S(2)}, u32[]{:S(2)}) async-start(bf16[128,2,32,128]{3,2,1,0:T(8,128)(2,1)} %bitcast.16), calls=%async_computation | async-start | bytes 4194304 | tf_op jit(solution)/shard_map/all_to_all | solution.py:310
  23.8 1.3 %copy-start = (f32[32,128,128]{2,1,0:T(8,128)}, f32[32,128,128]{2,1,0:T(8,128)S(1)}, u32[]{:S(2)}) copy-start(f32[32,128,128]{2,1,0:T(8,128)S(1)} %gates.1) | copy-start | bytes 6291460
  73.0 5.0 %collective-permute-start = (bf16[16,8,32,128]{3,2,1,0:T(8,128)(2,1)S(1)}, bf16[16,8,32,128]{3,2,1,0:T(8,128)(2,1)S(1)}, u32[]{:S(2)}, u32[]{:S(2)}) collective-permute-start(bf16[16,8,32,128]{3,2,1,0:T(8,128)(2,1)S(1)} %split.1), channel_id=1, source_target_pairs={{0,8},{8,0},{1,9},{9,1},{2,10},{10,2},{3,11},{11,3},{4,12},{12,4},... | collective-permute-start | bytes 3145736 | tf_op jit(solution)/shard_map/ppermute | solution.py:314
  78.0 37.2 %copy-start.1 = (f32[32,128,128]{2,1,0:T(8,128)S(1)}, f32[32,128,128]{2,1,0:T(8,128)}, u32[]{:S(2)}) copy-start(f32[32,128,128]{2,1,0:T(8,128)} %copy-done) | copy-start | bytes 6291460
  78.0 37.2 %copy-start.4 = (bf16[128,128]{1,0:T(8,128)(2,1)S(1)}, bf16[128,128]{1,0:T(8,128)(2,1)}, u32[]{:S(2)}) copy-start(bf16[128,128]{1,0:T(8,128)(2,1)} %weight_ref.3) | copy-start | bytes 98308
  78.0 37.3 %copy-start.6 = (f32[128]{0:T(128)S(1)}, f32[128]{0:T(128)}, u32[]{:S(2)}) copy-start(f32[128]{0:T(128)} %param.12) | copy-start | bytes 1540
  79.8 35.4 %all-to-all-start.1 = ((bf16[128,32,128]{2,1,0:T(8,128)(2,1)}), bf16[128,32,128]{2,1,0:T(8,128)(2,1)S(1)}, u32[]{:S(2)}, u32[]{:S(2)}) async-start(bf16[128,32,128]{2,1,0:T(8,128)(2,1)} %bitcast.17), calls=%async_computation.1 | async-start | bytes 2097152 | tf_op jit(solution)/shard_map/all_to_all | solution.py:317

commit v8 on v4

--- a/solution.py
+++ b/solution.py
@@ -15,10 +15,10 @@
     return 0.5 * jnp.tanh(0.5 * values) + 0.5
 
 
-def normalize(values, gain):
-    average = jnp.mean(values, axis=-1, keepdims=True)
+def normalize(values, gain, axis):
+    average = jnp.mean(values, axis=axis, keepdims=True)
     centered = values - average
-    spread = jnp.mean(centered * centered, axis=-1, keepdims=True)
+    spread = jnp.mean(centered * centered, axis=axis, keepdims=True)
     return (centered * lax.rsqrt(spread + 1e-05) * gain).astype(BF16)
 
 
@@ -49,16 +49,16 @@
         copy.wait()
     for side in range(2):
         turned[side * wide : (side + 1) * wide] = (0.5 * weights[side].astype(F32)).T.astype(BF16)
-    gain = gain_ref[...]
+    gain = jnp.broadcast_to(gain_ref[...], (2 * here_k, channels)).T
     for core in range(cores):
         for i in range(0, half, 2):
             row = core * half + i
             if row % part == 0:
                 pieces[row // part].wait()
-            rows = pair_ref[row : row + 2].reshape(2 * here_k, channels).astype(F32)
-            normed = normalize(rows, gain)
+            turned_rows = pair_ref[row : row + 2].reshape(2 * here_k, channels).T.astype(F32)
+            normed = normalize(turned_rows, gain, 0)
             both = lax.dot_general(
-                turned[...], normed, (((1,), (1,)), ((), ())), preferred_element_type=F32
+                turned[...], normed, (((1,), (0,)), ((), ())), preferred_element_type=F32
             )
             for side in range(2):
                 one = both[side * wide : (side + 1) * wide]
@@ -201,7 +201,7 @@
 def gate_kernel(pair_ref, gain_ref, weight_ref, gate_ref):
     some, here_k, channels = pair_ref.shape
     rows = pair_ref[...].reshape(some * here_k, channels).astype(F32)
-    normed = normalize(rows, gain_ref[...])
+    normed = normalize(rows, gain_ref[...], 1)
     gate = sigmoid(jnp.dot(normed, weight_ref[...], preferred_element_type=F32))
     gate_ref[...] = gate.reshape(gate_ref.shape)
 

time: 117 us -> 117 us (level)
  no operation moved by 1% of the time
where the time goes in v8:
time: 117 us
  blocking collectives  68.6 us (59%)
  waiting for transfers between devices  28.9 us (25%)
  Pallas kernels  11.2 us (10%)
  starting transfers between devices  6.74 us (6%)
  local copies, waits for them, and re-layouts  1.24 us (1%)
    all_to_all x1, blocking collectives, shards(): got = exchange(sent.reshape(rows * cols, 2, half, here_k))  68.6 us
    all_to_all x1, waiting for transfers between devices, shards(): back = exchange(product.reshape(rows * cols, half, here_k))  27.1 us
    all_to_all x1, starting transfers between devices, shards(): back = exchange(product.reshape(rows * cols, half, here_k))  6.65 us
    pallas_call x1, Pallas kernels, operands(): pl.pallas_call(operands_kernel, in_specs=[hbm] * 4, out_specs=pl.BlockSpe...  4.14 us
    pallas_call x1, Pallas kernels, updates(): pl.pallas_call(update_kernel, in_specs=[pl.BlockSpec(memory_space=pltpu.S...  2.38 us
  transfers between devices with their start and end apart: 2, of which 2 were waited for; matrix products, arithmetic and copies ran while one was open for 0% of the time, Pallas kernels for 2%

profile of v8, /device:TPU:1, one launch (start us, length us, event | category | flops | bytes accessed | tf_op | source)
XLA Modules:
  0.0 116.8 jit_solution(4470060015509612428)
XLA Ops:
  0.0 4.1 %operands.1 = bf16[16,2,8,2,16,128]{5,4,3,2,1,0:T(8,128)(2,1)S(1)} custom-call(bf16[32,128,128]{2,1,0:T(8,128)(2,1)} %pair_ref, f32[1,128]{1,0:T(1,128)} %bitcast.14, bf16[128,256]{1,0:T(8,128)(2,1)} %left_hbm.1, bf16[128,256]{1,0:T(8,128)(2,1)} %right_hbm.1), custom_call_target="tpu_custom_call" | custom-call | tf_op jit(solution)/shard_map/operands/pallas_call | solution.py:81
  4.2 68.6 %all_to_all.10 = bf16[256,2,16,128]{3,2,1,0:T(8,128)(2,1)S(1)} all-to-all(bf16[256,2,16,128]{3,2,1,0:T(8,128)(2,1)S(1)} %bitcast.12), channel_id=1, replica_groups=mesh['row'=32,'col'=8] {'row','col'}, dimensions={0} | all-to-all | bytes 4194304 | tf_op jit(solution)/shard_map/all_to_all | solution.py:297
  72.7 0.1 split.1
  72.8 0.1 collective-permute-start
  72.9 0.8 own_part.1
  73.7 1.8 %collective-permute-done.other_ref = bf16[32,8,16,128]{3,2,1,0:T(8,128)(2,1)S(1)} collective-permute-done((bf16[32,8,16,128]{3,2,1,0:T(8,128)(2,1)S(1)}, bf16[32,8,16,128]{3,2,1,0:T(8,128)(2,1)S(1)}, u32[]{:S(2)}, u32[]{:S(2)}) %collective-permute-start) | collective-permute-done | bytes 1048608 | tf_op jit(solution)/shard_map/ppermute | solution.py:299
  75.6 0.0 copy-start.1
  75.6 0.0 copy-start.3
  75.6 1.8 %merge.1 = bf16[32,8,16,128]{3,2,1,0:T(8,128)(2,1)} custom-call(bf16[512,1024]{1,0:T(8,128)(2,1)S(1)} %get-tuple-element.9.left_ref, bf16[512,512]{1,0:T(8,128)(2,1)S(1)} %get-tuple-element.10.own_ref, bf16[32,8,16,128]{3,2,1,0:T(8,128)(2,1)S(1)} %collective-permute-done.other_ref), custom_call_target="tpu_custom_call" | custom-call | tf_op jit(solution)/shard_map/merge/pallas_call | solution.py:186
  77.4 0.0 copy-start.2
  77.4 6.7 %all-to-all-start.1 = ((bf16[256,16,128]{2,1,0:T(8,128)(2,1)}), bf16[256,16,128]{2,1,0:T(8,128)(2,1)S(1)}, u32[]{:S(2)}, u32[]{:S(2)}) async-start(bf16[256,16,128]{2,1,0:T(8,128)(2,1)} %bitcast.4), calls=%async_computation.1 | async-start | bytes 2097152 | tf_op jit(solution)/shard_map/all_to_all | solution.py:303
  84.0 0.0 copy-start.4
  84.1 0.0 copy-done.1
  84.1 0.0 copy-done.3
  84.1 0.0 copy-start
  84.1 1.2 %copy-done = bf16[32,128,128]{2,1,0:T(8,128)(2,1)S(1)} copy-done((bf16[32,128,128]{2,1,0:T(8,128)(2,1)S(1)}, bf16[32,128,128]{2,1,0:T(8,128)(2,1)}, u32[]{:S(2)}) %copy-start) | copy-done | bytes 1048600
  85.3 2.0 %gates.1 = f32[32,128,128]{2,1,0:T(8,128)S(1)} custom-call(bf16[32,128,128]{2,1,0:T(8,128)(2,1)S(1)} %copy-done, f32[1,128]{1,0:T(1,128)S(1)} %bitcast.15, bf16[128,128]{1,0:T(8,128)(2,1)S(1)} %copy-done.1), custom_call_target="tpu_custom_call" | custom-call | flops 134217728 | bytes 3145728 | tf_op jit(solution)/shard_map/gates/pallas_call | solution.py:213
  87.3 27.1 %all-to-all-done.1 = bf16[256,16,128]{2,1,0:T(8,128)(2,1)S(1)} async-done(((bf16[256,16,128]{2,1,0:T(8,128)(2,1)}), bf16[256,16,128]{2,1,0:T(8,128)(2,1)S(1)}, u32[]{:S(2)}, u32[]{:S(2)}) %all-to-all-start.1) | async-done | bytes 1048608 | tf_op jit(solution)/shard_map/all_to_all | solution.py:303
  114.4 0.0 copy-done.2
  114.4 0.0 copy-done.4
  114.4 2.4 %updates.1 = bf16[32,4,2,16,128]{4,3,2,1,0:T(8,128)(2,1)} custom-call(s32[1]{0:T(128)} %bitcast.odd_ref, bf16[16,2,8,16,128]{4,3,2,1,0:T(8,128)(2,1)S(1)} %bitcast.13, f32[1,128]{1,0:T(1,128)S(1)} %bitcast.16, bf16[128,128]{1,0:T(8,128)(2,1)S(1)} %copy-done.2, f32[32,4,2,16,128]{4,3,2,1,0:T(8,128)S(1)} %bitcast.11), custom_call_target="tpu_custom_call" | custom-call | tf_op jit(solution)/shard_map/updates/pallas_call | solution.py:272
Async XLA Ops:
  72.8 2.7 %collective-permute-start = (bf16[32,8,16,128]{3,2,1,0:T(8,128)(2,1)S(1)}, bf16[32,8,16,128]{3,2,1,0:T(8,128)(2,1)S(1)}, u32[]{:S(2)}, u32[]{:S(2)}) collective-permute-start(bf16[32,8,16,128]{3,2,1,0:T(8,128)(2,1)S(1)} %split.1), channel_id=1, source_target_pairs={{0,8},{8,0},{16,24},{24,16},{32,40},{40,32},{48,56},{56,48},{64,72... | collective-permute-start | bytes 3145736 | tf_op jit(solution)/shard_map/ppermute | solution.py:299
  75.6 8.5 %copy-start.1 = (bf16[128,128]{1,0:T(8,128)(2,1)S(1)}, bf16[128,128]{1,0:T(8,128)(2,1)}, u32[]{:S(2)}) copy-start(bf16[128,128]{1,0:T(8,128)(2,1)} %weight_ref.2) | copy-start | bytes 98308
  75.6 8.5 %copy-start.3 = (f32[128]{0:T(128)S(1)}, f32[128]{0:T(128)}, u32[]{:S(2)}) copy-start(f32[128]{0:T(128)} %param.8) | copy-start | bytes 1540
  77.4 37.0 %copy-start.2 = (bf16[128,128]{1,0:T(8,128)(2,1)S(1)}, bf16[128,128]{1,0:T(8,128)(2,1)}, u32[]{:S(2)}) copy-start(bf16[128,128]{1,0:T(8,128)(2,1)} %weight_ref.3) | copy-start | bytes 98308
  77.4 37.0 %all-to-all-start.1 = ((bf16[256,16,128]{2,1,0:T(8,128)(2,1)}), bf16[256,16,128]{2,1,0:T(8,128)(2,1)S(1)}, u32[]{:S(2)}, u32[]{:S(2)}) async-start(bf16[256,16,128]{2,1,0:T(8,128)(2,1)} %bitcast.4), calls=%async_computation.1 | async-start | bytes 2097152 | tf_op jit(solution)/shard_map/all_to_all | solution.py:303
  84.0 30.4 %copy-start.4 = (f32[128]{0:T(128)S(1)}, f32[128]{0:T(128)}, u32[]{:S(2)}) copy-start(f32[128]{0:T(128)} %param.12) | copy-start | bytes 1540
  84.1 1.2 %copy-start = (bf16[32,128,128]{2,1,0:T(8,128)(2,1)S(1)}, bf16[32,128,128]{2,1,0:T(8,128)(2,1)}, u32[]{:S(2)}) copy-start(bf16[32,128,128]{2,1,0:T(8,128)(2,1)} %pair_ref) | copy-start | bytes 3145732

commit v9 on v8

--- a/solution.py
+++ b/solution.py
@@ -22,7 +22,7 @@
     return (centered * lax.rsqrt(spread + 1e-05) * gain).astype(BF16)
 
 
-PARTS = 4
+PARTS = 2
 
 
 def operands_kernel(
@@ -235,7 +235,7 @@
     width, each = chips * cols, gate_ref.shape[1]
     channels = gate_ref.shape[4]
     odd = odd_ref[0]
-    gain = jnp.broadcast_to(gain_ref[...], (here_k, width)).T
+    gain = jnp.broadcast_to(gain_ref[...], (here_k, width)).T.reshape(width, 1, here_k)
     outgoing = []
     for c in range(cores):
         product = back_ref[:, c].reshape(width, half, here_k).astype(F32)
@@ -243,7 +243,7 @@
         centered = product - average
         spread = jnp.mean(centered * centered, axis=0, keepdims=True)
         normed = centered * lax.rsqrt(spread + 1e-05)
-        normed = (jnp.swapaxes(normed, 0, 1) * gain).astype(BF16)
+        normed = jnp.swapaxes((normed * gain).astype(BF16), 0, 1)
         first = (c + odd) % 2
         for i in range(half):
             row = c * half + i

time: 117 us -> 116 us (level)
  no operation moved by 1% of the time
where the time goes in v9:
time: 116 us
  blocking collectives  68.6 us (59%)
  waiting for transfers between devices  28.9 us (25%)
  Pallas kernels  10.3 us (9%)
  starting transfers between devices  6.74 us (6%)
  local copies, waits for them, and re-layouts  1.24 us (1%)
    all_to_all x1, blocking collectives, shards(): got = exchange(sent.reshape(rows * cols, 2, half, here_k))  68.6 us
    all_to_all x1, waiting for transfers between devices, shards(): back = exchange(product.reshape(rows * cols, half, here_k))  27.1 us
    all_to_all x1, starting transfers between devices, shards(): back = exchange(product.reshape(rows * cols, half, here_k))  6.65 us
    pallas_call x1, Pallas kernels, operands(): pl.pallas_call(operands_kernel, in_specs=[hbm] * 4, out_specs=pl.BlockSpe...  3.55 us
  transfers between devices with their start and end apart: 2, of which 2 were waited for; matrix products, arithmetic and copies ran while one was open for 0% of the time, Pallas kernels for 2%

profile of v9, /device:TPU:1, one launch (start us, length us, event | category | flops | bytes accessed | tf_op | source)
XLA Modules:
  0.0 115.9 jit_solution(10418945193725136354)
XLA Ops:
  0.0 3.6 %operands.1 = bf16[16,2,8,2,16,128]{5,4,3,2,1,0:T(8,128)(2,1)S(1)} custom-call(bf16[32,128,128]{2,1,0:T(8,128)(2,1)} %pair_ref, f32[1,128]{1,0:T(1,128)} %bitcast.14, bf16[128,256]{1,0:T(8,128)(2,1)} %left_hbm.1, bf16[128,256]{1,0:T(8,128)(2,1)} %right_hbm.1), custom_call_target="tpu_custom_call" | custom-call | tf_op jit(solution)/shard_map/operands/pallas_call | solution.py:81
  3.6 68.6 %all_to_all.10 = bf16[256,2,16,128]{3,2,1,0:T(8,128)(2,1)S(1)} all-to-all(bf16[256,2,16,128]{3,2,1,0:T(8,128)(2,1)S(1)} %bitcast.12), channel_id=1, replica_groups=mesh['row'=32,'col'=8] {'row','col'}, dimensions={0} | all-to-all | bytes 4194304 | tf_op jit(solution)/shard_map/all_to_all | solution.py:297
  72.1 0.1 split.1
  72.2 0.1 collective-permute-start
  72.3 0.8 own_part.1
  73.1 1.8 %collective-permute-done.other_ref = bf16[32,8,16,128]{3,2,1,0:T(8,128)(2,1)S(1)} collective-permute-done((bf16[32,8,16,128]{3,2,1,0:T(8,128)(2,1)S(1)}, bf16[32,8,16,128]{3,2,1,0:T(8,128)(2,1)S(1)}, u32[]{:S(2)}, u32[]{:S(2)}) %collective-permute-start) | collective-permute-done | bytes 1048608 | tf_op jit(solution)/shard_map/ppermute | solution.py:299
  75.0 0.0 copy-start.1
  75.0 0.0 copy-start.3
  75.0 1.8 %merge.1 = bf16[32,8,16,128]{3,2,1,0:T(8,128)(2,1)} custom-call(bf16[512,1024]{1,0:T(8,128)(2,1)S(1)} %get-tuple-element.9.left_ref, bf16[512,512]{1,0:T(8,128)(2,1)S(1)} %get-tuple-element.10.own_ref, bf16[32,8,16,128]{3,2,1,0:T(8,128)(2,1)S(1)} %collective-permute-done.other_ref), custom_call_target="tpu_custom_call" | custom-call | tf_op jit(solution)/shard_map/merge/pallas_call | solution.py:186
  76.8 0.0 copy-start.2
  76.8 6.7 %all-to-all-start.1 = ((bf16[256,16,128]{2,1,0:T(8,128)(2,1)}), bf16[256,16,128]{2,1,0:T(8,128)(2,1)S(1)}, u32[]{:S(2)}, u32[]{:S(2)}) async-start(bf16[256,16,128]{2,1,0:T(8,128)(2,1)} %bitcast.4), calls=%async_computation.1 | async-start | bytes 2097152 | tf_op jit(solution)/shard_map/all_to_all | solution.py:303
  83.4 0.0 copy-start.4
  83.5 0.0 copy-done.1
  83.5 0.0 copy-done.3
  83.5 0.0 copy-start
  83.5 1.2 %copy-done = bf16[32,128,128]{2,1,0:T(8,128)(2,1)S(1)} copy-done((bf16[32,128,128]{2,1,0:T(8,128)(2,1)S(1)}, bf16[32,128,128]{2,1,0:T(8,128)(2,1)}, u32[]{:S(2)}) %copy-start) | copy-done | bytes 1048600
  84.7 2.0 %gates.1 = f32[32,128,128]{2,1,0:T(8,128)S(1)} custom-call(bf16[32,128,128]{2,1,0:T(8,128)(2,1)S(1)} %copy-done, f32[1,128]{1,0:T(1,128)S(1)} %bitcast.15, bf16[128,128]{1,0:T(8,128)(2,1)S(1)} %copy-done.1), custom_call_target="tpu_custom_call" | custom-call | flops 134217728 | bytes 3145728 | tf_op jit(solution)/shard_map/gates/pallas_call | solution.py:213
  86.7 27.1 %all-to-all-done.1 = bf16[256,16,128]{2,1,0:T(8,128)(2,1)S(1)} async-done(((bf16[256,16,128]{2,1,0:T(8,128)(2,1)}), bf16[256,16,128]{2,1,0:T(8,128)(2,1)S(1)}, u32[]{:S(2)}, u32[]{:S(2)}) %all-to-all-start.1) | async-done | bytes 1048608 | tf_op jit(solution)/shard_map/all_to_all | solution.py:303
  113.8 0.0 copy-done.2
  113.8 0.0 copy-done.4
  113.8 2.1 %updates.1 = bf16[32,4,2,16,128]{4,3,2,1,0:T(8,128)(2,1)} custom-call(s32[1]{0:T(128)} %bitcast.odd_ref, bf16[16,2,8,16,128]{4,3,2,1,0:T(8,128)(2,1)S(1)} %bitcast.13, f32[1,128]{1,0:T(1,128)S(1)} %bitcast.16, bf16[128,128]{1,0:T(8,128)(2,1)S(1)} %copy-done.2, f32[32,4,2,16,128]{4,3,2,1,0:T(8,128)S(1)} %bitcast.11), custom_call_target="tpu_custom_call" | custom-call | tf_op jit(solution)/shard_map/updates/pallas_call | solution.py:272
Async XLA Ops:
  72.2 2.7 %collective-permute-start = (bf16[32,8,16,128]{3,2,1,0:T(8,128)(2,1)S(1)}, bf16[32,8,16,128]{3,2,1,0:T(8,128)(2,1)S(1)}, u32[]{:S(2)}, u32[]{:S(2)}) collective-permute-start(bf16[32,8,16,128]{3,2,1,0:T(8,128)(2,1)S(1)} %split.1), channel_id=1, source_target_pairs={{0,8},{8,0},{16,24},{24,16},{32,40},{40,32},{48,56},{56,48},{64,72... | collective-permute-start | bytes 3145736 | tf_op jit(solution)/shard_map/ppermute | solution.py:299
  75.0 8.5 %copy-start.1 = (bf16[128,128]{1,0:T(8,128)(2,1)S(1)}, bf16[128,128]{1,0:T(8,128)(2,1)}, u32[]{:S(2)}) copy-start(bf16[128,128]{1,0:T(8,128)(2,1)} %weight_ref.2) | copy-start | bytes 98308
  75.0 8.5 %copy-start.3 = (f32[128]{0:T(128)S(1)}, f32[128]{0:T(128)}, u32[]{:S(2)}) copy-start(f32[128]{0:T(128)} %param.8) | copy-start | bytes 1540
  76.8 37.0 %copy-start.2 = (bf16[128,128]{1,0:T(8,128)(2,1)S(1)}, bf16[128,128]{1,0:T(8,128)(2,1)}, u32[]{:S(2)}) copy-start(bf16[128,128]{1,0:T(8,128)(2,1)} %weight_ref.3) | copy-start | bytes 98308
  76.8 37.0 %all-to-all-start.1 = ((bf16[256,16,128]{2,1,0:T(8,128)(2,1)}), bf16[256,16,128]{2,1,0:T(8,128)(2,1)S(1)}, u32[]{:S(2)}, u32[]{:S(2)}) async-start(bf16[256,16,128]{2,1,0:T(8,128)(2,1)} %bitcast.4), calls=%async_computation.1 | async-start | bytes 2097152 | tf_op jit(solution)/shard_map/all_to_all | solution.py:303
  83.4 30.4 %copy-start.4 = (f32[128]{0:T(128)S(1)}, f32[128]{0:T(128)}, u32[]{:S(2)}) copy-start(f32[128]{0:T(128)} %param.12) | copy-start | bytes 1540
  83.5 1.2 %copy-start = (bf16[32,128,128]{2,1,0:T(8,128)(2,1)S(1)}, bf16[32,128,128]{2,1,0:T(8,128)(2,1)}, u32[]{:S(2)}) copy-start(bf16[32,128,128]{2,1,0:T(8,128)(2,1)} %pair_ref) | copy-start | bytes 3145732

commit v10 on v9

--- a/solution.py
+++ b/solution.py
@@ -45,7 +45,7 @@
     ]
     for copy in pieces[:1] + small + pieces[1:]:
         copy.start()
-    for copy in small:
+    for copy in small + pieces[:1]:
         copy.wait()
     for side in range(2):
         turned[side * wide : (side + 1) * wide] = (0.5 * weights[side].astype(F32)).T.astype(BF16)
@@ -53,7 +53,7 @@
     for core in range(cores):
         for i in range(0, half, 2):
             row = core * half + i
-            if row % part == 0:
+            if row % part == 0 and row > 0:
                 pieces[row // part].wait()
             turned_rows = pair_ref[row : row + 2].reshape(2 * here_k, channels).T.astype(F32)
             normed = normalize(turned_rows, gain, 0)
@@ -97,7 +97,9 @@
 
 
 def split_kernel(got_ref, right_ref):
-    right_ref[...] = got_ref[:, :, 1]
+    rows, cols, _, half, here_k = got_ref.shape
+    for s in range(cols):
+        right_ref[:, s * here_k : (s + 1) * here_k] = got_ref[:, s, 1].reshape(rows * half, here_k)
 
 
 def split(got):
@@ -107,58 +109,56 @@
         split_kernel,
         in_specs=[vmem],
         out_specs=vmem,
-        out_shape=jax.ShapeDtypeStruct((rows, cols, half, here_k), BF16),
+        out_shape=jax.ShapeDtypeStruct((rows * half, cols * here_k), BF16),
         compiler_params=pltpu.CompilerParams(vmem_limit_bytes=VMEM_LIMIT),
         name="split",
     )(got)
 
 
-def own_kernel(got_ref, left_ref, own_ref, right):
+def own_kernel(got_ref, right_ref, left_ref, own_ref):
     rows, cols, _, half, here_k = got_ref.shape
     for s in range(cols):
         span = pl.ds(s * here_k, here_k)
         left_ref[:, span] = got_ref[:, s, 0].reshape(rows * half, here_k)
-        right[:, span] = got_ref[:, s, 1].reshape(rows * half, here_k)
     step = 2 * here_k
     for j in range(0, rows * half, step):
         own_ref[:, j : j + step] = lax.dot_general(
-            left_ref[...], right[j : j + step], (((1,), (1,)), ((), ())), preferred_element_type=F32
+            left_ref[...], right_ref[j : j + step], (((1,), (1,)), ((), ())), preferred_element_type=F32
         ).astype(BF16)
 
 
-def own_part(got):
+def own_part(got, right):
     rows, cols, _, half, here_k = got.shape
     tall, deep = rows * half, cols * here_k
     vmem = pl.BlockSpec(memory_space=pltpu.VMEM)
     return pl.pallas_call(
         own_kernel,
-        in_specs=[vmem],
+        in_specs=[vmem, vmem],
         out_specs=[vmem, vmem],
         out_shape=[
             jax.ShapeDtypeStruct((tall, deep), BF16),
             jax.ShapeDtypeStruct((tall, tall), BF16),
         ],
-        scratch_shapes=[pltpu.VMEM((tall, deep), BF16)],
         compiler_params=pltpu.CompilerParams(vmem_limit_bytes=VMEM_LIMIT),
         cost_estimate=pl.CostEstimate(
             flops=2 * tall * tall * deep, bytes_accessed=8 * tall * deep, transcendentals=0
         ),
         name="own_part",
-    )(got)
-
-
-def merge_kernel(left_ref, own_ref, other_ref, product_hbm, product_ref, right, left):
-    rows, cols, half, here_k = other_ref.shape
+    )(got, right)
+
+
+def merge_kernel(left_ref, own_ref, other_ref, product_hbm, product_ref, left):
+    rows, cols, half, here_k = product_ref.shape
     each = rows // cols * half
-    for s in range(cols):
-        span = pl.ds(s * here_k, here_k)
-        block = other_ref[:, s].reshape(cols // 2, 2, each, here_k)
-        right[:, 1, :, span] = block[:, 0]
-        right[:, 0, :, span] = block[:, 1]
     outgoing = []
     first = lax.broadcasted_iota(jnp.int32, (1, here_k), 1) < each
     for pair in range(0, cols // 2, 2):
-        part = right[pair : pair + 2].reshape(2 * here_k, cols * here_k)
+        part = jnp.concatenate(
+            [
+                other_ref[s * each : (s + 1) * each]
+                for s in (2 * pair + 1, 2 * pair, 2 * pair + 3, 2 * pair + 2)
+            ]
+        )
         total = lax.dot_general(
             left_ref[...], part, (((1,), (1,)), ((), ())), preferred_element_type=F32
         )
@@ -180,17 +180,16 @@
         copy.wait()
 
 
-def merge(left, own, other):
-    rows, cols, half, here_k = other.shape
+def merge(left, own, other, shape):
+    cols = shape[1]
     vmem = pl.BlockSpec(memory_space=pltpu.VMEM)
     return pl.pallas_call(
         merge_kernel,
         in_specs=[vmem, vmem, vmem],
         out_specs=pl.BlockSpec(memory_space=pltpu.HBM),
-        out_shape=jax.ShapeDtypeStruct(other.shape, BF16),
+        out_shape=jax.ShapeDtypeStruct(shape, BF16),
         scratch_shapes=[
-            pltpu.VMEM(other.shape, BF16),
-            pltpu.VMEM((cols // 2, 2, rows // cols * half, cols * here_k), BF16),
+            pltpu.VMEM(shape, BF16),
             pltpu.SemaphoreType.DMA((cols // 2,)),
         ],
         compiler_params=pltpu.CompilerParams(vmem_limit_bytes=VMEM_LIMIT),
@@ -296,9 +295,10 @@
     sent = operands(pair, gain, proj_left, proj_right, chips, cols)
     got = exchange(sent.reshape(rows * cols, 2, half, here_k))
     got = got.reshape(rows, cols, 2, half, here_k)
-    other = lax.ppermute(split(got), "row", [(r, r ^ 1) for r in range(rows)])
-    left, own = own_part(got)
-    product = merge(left, own, other)
+    right = split(got)
+    other = lax.ppermute(right, "row", [(r, r ^ 1) for r in range(rows)])
+    left, own = own_part(got, right)
+    product = merge(left, own, other, (rows, cols, half, here_k))
     product, late_pair = lax.optimization_barrier((product, pair))
     back = exchange(product.reshape(rows * cols, half, here_k))
     gate = gates(late_pair, gain, gate_weight)

time: 116 us -> 116 us (level)
  no operation moved by 1% of the time
where the time goes in v10:
time: 116 us
  blocking collectives  68.6 us (59%)
  waiting for transfers between devices  29 us (25%)
  Pallas kernels  10.2 us (9%)
  starting transfers between devices  6.74 us (6%)
  local copies, waits for them, and re-layouts  1.24 us (1%)
    all_to_all x1, blocking collectives, shards(): got = exchange(sent.reshape(rows * cols, 2, half, here_k))  68.6 us
    all_to_all x1, waiting for transfers between devices, shards(): back = exchange(product.reshape(rows * cols, half, here_k))  27.1 us
    all_to_all x1, starting transfers between devices, shards(): back = exchange(product.reshape(rows * cols, half, here_k))  6.65 us
    pallas_call x1, Pallas kernels, operands(): pl.pallas_call(operands_kernel, in_specs=[hbm] * 4, out_specs=pl.BlockSpe...  3.41 us
  transfers between devices with their start and end apart: 2, of which 2 were waited for; matrix products, arithmetic and copies ran while one was open for 0% of the time, Pallas kernels for 2%

profile of v10, /device:TPU:1, one launch (start us, length us, event | category | flops | bytes accessed | tf_op | source)
XLA Modules:
  0.0 115.9 jit_solution(15756390095613363827)
XLA Ops:
  0.0 3.4 %operands.1 = bf16[16,2,8,2,16,128]{5,4,3,2,1,0:T(8,128)(2,1)S(1)} custom-call(bf16[32,128,128]{2,1,0:T(8,128)(2,1)} %pair_ref, f32[1,128]{1,0:T(1,128)} %bitcast.14, bf16[128,256]{1,0:T(8,128)(2,1)} %left_hbm.1, bf16[128,256]{1,0:T(8,128)(2,1)} %right_hbm.1), custom_call_target="tpu_custom_call" | custom-call | tf_op jit(solution)/shard_map/operands/pallas_call | solution.py:81
  3.4 68.6 %all_to_all.10 = bf16[256,2,16,128]{3,2,1,0:T(8,128)(2,1)S(1)} all-to-all(bf16[256,2,16,128]{3,2,1,0:T(8,128)(2,1)S(1)} %bitcast.12), channel_id=1, replica_groups=mesh['row'=32,'col'=8] {'row','col'}, dimensions={0} | all-to-all | bytes 4194304 | tf_op jit(solution)/shard_map/all_to_all | solution.py:296
  72.0 0.3 split.1.right_ref
  72.3 0.1 collective-permute-start
  72.4 0.8 own_part.1
  73.2 1.9 %collective-permute-done.other_ref = bf16[512,1024]{1,0:T(8,128)(2,1)S(1)} collective-permute-done((bf16[512,1024]{1,0:T(8,128)(2,1)S(1)}, bf16[512,1024]{1,0:T(8,128)(2,1)S(1)}, u32[]{:S(2)}, u32[]{:S(2)}) %collective-permute-start) | collective-permute-done | bytes 1048608 | tf_op jit(solution)/shard_map/ppermute | solution.py:299
  75.0 0.0 copy-start.1
  75.0 0.0 copy-start.3
  75.0 1.7 %merge.1 = bf16[32,8,16,128]{3,2,1,0:T(8,128)(2,1)} custom-call(bf16[512,1024]{1,0:T(8,128)(2,1)S(1)} %get-tuple-element.9.left_ref, bf16[512,512]{1,0:T(8,128)(2,1)S(1)} %get-tuple-element.10.own_ref, bf16[512,1024]{1,0:T(8,128)(2,1)S(1)} %collective-permute-done.other_ref), custom_call_target="tpu_custom_call" | custom-call | tf_op jit(solution)/shard_map/merge/pallas_call | solution.py:186
  76.8 0.0 copy-start.2
  76.8 6.6 %all-to-all-start.1 = ((bf16[256,16,128]{2,1,0:T(8,128)(2,1)}), bf16[256,16,128]{2,1,0:T(8,128)(2,1)S(1)}, u32[]{:S(2)}, u32[]{:S(2)}) async-start(bf16[256,16,128]{2,1,0:T(8,128)(2,1)} %bitcast.4), calls=%async_computation.1 | async-start | bytes 2097152 | tf_op jit(solution)/shard_map/all_to_all | solution.py:303
  83.5 0.0 copy-start.4
  83.5 0.0 copy-done.1
  83.5 0.0 copy-done.3
  83.5 0.0 copy-start
  83.5 1.2 %copy-done = bf16[32,128,128]{2,1,0:T(8,128)(2,1)S(1)} copy-done((bf16[32,128,128]{2,1,0:T(8,128)(2,1)S(1)}, bf16[32,128,128]{2,1,0:T(8,128)(2,1)}, u32[]{:S(2)}) %copy-start) | copy-done | bytes 1048600
  84.7 2.0 %gates.1 = f32[32,128,128]{2,1,0:T(8,128)S(1)} custom-call(bf16[32,128,128]{2,1,0:T(8,128)(2,1)S(1)} %copy-done, f32[1,128]{1,0:T(1,128)S(1)} %bitcast.15, bf16[128,128]{1,0:T(8,128)(2,1)S(1)} %copy-done.1), custom_call_target="tpu_custom_call" | custom-call | flops 134217728 | bytes 3145728 | tf_op jit(solution)/shard_map/gates/pallas_call | solution.py:212
  86.7 27.1 %all-to-all-done.1 = bf16[256,16,128]{2,1,0:T(8,128)(2,1)S(1)} async-done(((bf16[256,16,128]{2,1,0:T(8,128)(2,1)}), bf16[256,16,128]{2,1,0:T(8,128)(2,1)S(1)}, u32[]{:S(2)}, u32[]{:S(2)}) %all-to-all-start.1) | async-done | bytes 1048608 | tf_op jit(solution)/shard_map/all_to_all | solution.py:303
  113.8 0.0 copy-done.2
  113.8 0.0 copy-done.4
  113.8 2.1 %updates.1 = bf16[32,4,2,16,128]{4,3,2,1,0:T(8,128)(2,1)} custom-call(s32[1]{0:T(128)} %bitcast.odd_ref, bf16[16,2,8,16,128]{4,3,2,1,0:T(8,128)(2,1)S(1)} %bitcast.13, f32[1,128]{1,0:T(1,128)S(1)} %bitcast.16, bf16[128,128]{1,0:T(8,128)(2,1)S(1)} %copy-done.2, f32[32,4,2,16,128]{4,3,2,1,0:T(8,128)S(1)} %bitcast.11), custom_call_target="tpu_custom_call" | custom-call | tf_op jit(solution)/shard_map/updates/pallas_call | solution.py:271
Async XLA Ops:
  72.3 2.7 %collective-permute-start = (bf16[512,1024]{1,0:T(8,128)(2,1)S(1)}, bf16[512,1024]{1,0:T(8,128)(2,1)S(1)}, u32[]{:S(2)}, u32[]{:S(2)}) collective-permute-start(bf16[512,1024]{1,0:T(8,128)(2,1)S(1)} %split.1.right_ref), channel_id=1, source_target_pairs={{0,8},{8,0},{16,24},{24,16},{32,40},{40,32},{48,56},{56,48},{64,72... | collective-permute-start | bytes 3145736 | tf_op jit(solution)/shard_map/ppermute | solution.py:299
  75.0 8.4 %copy-start.1 = (bf16[128,128]{1,0:T(8,128)(2,1)S(1)}, bf16[128,128]{1,0:T(8,128)(2,1)}, u32[]{:S(2)}) copy-start(bf16[128,128]{1,0:T(8,128)(2,1)} %weight_ref.2) | copy-start | bytes 98308
  75.0 8.5 %copy-start.3 = (f32[128]{0:T(128)S(1)}, f32[128]{0:T(128)}, u32[]{:S(2)}) copy-start(f32[128]{0:T(128)} %param.8) | copy-start | bytes 1540
  76.8 37.0 %copy-start.2 = (bf16[128,128]{1,0:T(8,128)(2,1)S(1)}, bf16[128,128]{1,0:T(8,128)(2,1)}, u32[]{:S(2)}) copy-start(bf16[128,128]{1,0:T(8,128)(2,1)} %weight_ref.3) | copy-start | bytes 98308
  76.8 37.0 %all-to-all-start.1 = ((bf16[256,16,128]{2,1,0:T(8,128)(2,1)}), bf16[256,16,128]{2,1,0:T(8,128)(2,1)S(1)}, u32[]{:S(2)}, u32[]{:S(2)}) async-start(bf16[256,16,128]{2,1,0:T(8,128)(2,1)} %bitcast.4), calls=%async_computation.1 | async-start | bytes 2097152 | tf_op jit(solution)/shard_map/all_to_all | solution.py:303
  83.5 30.4 %copy-start.4 = (f32[128]{0:T(128)S(1)}, f32[128]{0:T(128)}, u32[]{:S(2)}) copy-start(f32[128]{0:T(128)} %param.12) | copy-start | bytes 1540
  83.5 1.2 %copy-start = (bf16[32,128,128]{2,1,0:T(8,128)(2,1)S(1)}, bf16[32,128,128]{2,1,0:T(8,128)(2,1)}, u32[]{:S(2)}) copy-start(bf16[32,128,128]{2,1,0:T(8,128)(2,1)} %pair_ref) | copy-start | bytes 3145732

commit v11 on v10

--- a/solution.py
+++ b/solution.py
@@ -9,10 +9,6 @@
 
 F32, BF16 = jnp.float32, jnp.bfloat16
 VMEM_LIMIT = 40 * 1024 * 1024
-
-
-def sigmoid(values):
-    return 0.5 * jnp.tanh(0.5 * values) + 0.5
 
 
 def normalize(values, gain, axis):
@@ -115,7 +111,25 @@
     )(got)
 
 
-def own_kernel(got_ref, right_ref, left_ref, own_ref):
+def own_kernel(
+    got_ref, right_ref, pair_hbm, gain_hbm, weight_hbm, last_gain_hbm, last_weight_hbm,
+    left_ref, own_ref, gate_ref, columns_ref, halved_ref,
+    pair_ref, gain_ref, weight_ref, last_gain_ref, last_weight_ref, arrived,
+):
+    incoming = [
+        pltpu.make_async_copy(source, target, arrived.at[n])
+        for n, (source, target) in enumerate(
+            (
+                (weight_hbm, weight_ref),
+                (gain_hbm, gain_ref),
+                (pair_hbm, pair_ref),
+                (last_gain_hbm, last_gain_ref),
+                (last_weight_hbm, last_weight_ref),
+            )
+        )
+    ]
+    for copy in incoming:
+        copy.start()
     rows, cols, _, half, here_k = got_ref.shape
     for s in range(cols):
         span = pl.ds(s * here_k, here_k)
@@ -125,32 +139,56 @@
         own_ref[:, j : j + step] = lax.dot_general(
             left_ref[...], right_ref[j : j + step], (((1,), (1,)), ((), ())), preferred_element_type=F32
         ).astype(BF16)
-
-
-def own_part(got, right):
+    for copy in incoming:
+        copy.wait()
+    weight = (0.5 * weight_ref[...].astype(F32)).astype(BF16)
+    halved_ref[...] = (0.5 * last_weight_ref[...].astype(F32)).astype(BF16)
+    columns_ref[...] = jnp.broadcast_to(last_gain_ref[...], columns_ref.shape[::-1]).T
+    here_i, _, channels = pair_ref.shape
+    for i in range(0, here_i, 4):
+        some = pair_ref[i : i + 4].reshape(4 * here_k, channels).astype(F32)
+        gate = jnp.dot(normalize(some, gain_ref[...], 1), weight, preferred_element_type=F32)
+        gate_ref[i : i + 4] = (jnp.tanh(gate) + 1.0).reshape(4, here_k, channels)
+
+
+def own_part(got, right, pair, gain, gate_weight, last_gain, last_weight):
     rows, cols, _, half, here_k = got.shape
     tall, deep = rows * half, cols * here_k
-    vmem = pl.BlockSpec(memory_space=pltpu.VMEM)
+    vmem, hbm = pl.BlockSpec(memory_space=pltpu.VMEM), pl.BlockSpec(memory_space=pltpu.HBM)
+    arrays = [
+        pltpu.with_memory_space_constraint(array, pltpu.HBM)
+        for array in (pair, gain, gate_weight, last_gain, last_weight)
+    ]
     return pl.pallas_call(
         own_kernel,
-        in_specs=[vmem, vmem],
-        out_specs=[vmem, vmem],
+        in_specs=[vmem] * 2 + [hbm] * 5,
+        out_specs=[vmem] * 5,
         out_shape=[
             jax.ShapeDtypeStruct((tall, deep), BF16),
             jax.ShapeDtypeStruct((tall, tall), BF16),
+            jax.ShapeDtypeStruct(pair.shape, F32),
+            jax.ShapeDtypeStruct((last_gain.shape[1], here_k), F32),
+            jax.ShapeDtypeStruct(last_weight.shape, BF16),
+        ],
+        scratch_shapes=[
+            pltpu.VMEM(pair.shape, BF16),
+            pltpu.VMEM(gain.shape, F32),
+            pltpu.VMEM(gate_weight.shape, BF16),
+            pltpu.VMEM(last_gain.shape, F32),
+            pltpu.VMEM(last_weight.shape, BF16),
+            pltpu.SemaphoreType.DMA((5,)),
         ],
         compiler_params=pltpu.CompilerParams(vmem_limit_bytes=VMEM_LIMIT),
         cost_estimate=pl.CostEstimate(
             flops=2 * tall * tall * deep, bytes_accessed=8 * tall * deep, transcendentals=0
         ),
         name="own_part",
-    )(got, right)
-
-
-def merge_kernel(left_ref, own_ref, other_ref, product_hbm, product_ref, left):
+    )(got, right, *arrays)
+
+
+def merge_kernel(left_ref, own_ref, other_ref, product_ref):
     rows, cols, half, here_k = product_ref.shape
     each = rows // cols * half
-    outgoing = []
     first = lax.broadcasted_iota(jnp.int32, (1, here_k), 1) < each
     for pair in range(0, cols // 2, 2):
         part = jnp.concatenate(
@@ -170,61 +208,18 @@
             odd = jnp.where(first, other, own).astype(BF16)
             product_ref[:, 2 * (pair + p)] = even.reshape(rows, half, here_k)
             product_ref[:, 2 * (pair + p) + 1] = odd.reshape(rows, half, here_k)
-            span = pl.ds(2 * (pair + p), 2)
-            copy = pltpu.make_async_copy(
-                product_ref.at[:, span], product_hbm.at[:, span], left.at[pair + p]
-            )
-            copy.start()
-            outgoing.append(copy)
-    for copy in outgoing:
-        copy.wait()
 
 
 def merge(left, own, other, shape):
-    cols = shape[1]
     vmem = pl.BlockSpec(memory_space=pltpu.VMEM)
     return pl.pallas_call(
         merge_kernel,
         in_specs=[vmem, vmem, vmem],
-        out_specs=pl.BlockSpec(memory_space=pltpu.HBM),
+        out_specs=vmem,
         out_shape=jax.ShapeDtypeStruct(shape, BF16),
-        scratch_shapes=[
-            pltpu.VMEM(shape, BF16),
-            pltpu.SemaphoreType.DMA((cols // 2,)),
-        ],
         compiler_params=pltpu.CompilerParams(vmem_limit_bytes=VMEM_LIMIT),
         name="merge",
     )(left, own, other)
-
-
-def gate_kernel(pair_ref, gain_ref, weight_ref, gate_ref):
-    some, here_k, channels = pair_ref.shape
-    rows = pair_ref[...].reshape(some * here_k, channels).astype(F32)
-    normed = normalize(rows, gain_ref[...], 1)
-    gate = sigmoid(jnp.dot(normed, weight_ref[...], preferred_element_type=F32))
-    gate_ref[...] = gate.reshape(gate_ref.shape)
-
-
-def gates(pair, gain, weight):
-    here_i, here_k, channels = pair.shape
-    some = here_i // 4
-    block = pl.BlockSpec((some, here_k, channels), lambda i: (i, 0, 0))
-    return pl.pallas_call(
-        gate_kernel,
-        grid=(4,),
-        in_specs=[
-            block,
-            pl.BlockSpec(gain.shape, lambda i: (0, 0)),
-            pl.BlockSpec(weight.shape, lambda i: (0, 0)),
-        ],
-        out_specs=block,
-        out_shape=jax.ShapeDtypeStruct(pair.shape, F32),
-        compiler_params=pltpu.CompilerParams(vmem_limit_bytes=VMEM_LIMIT),
-        cost_estimate=pl.CostEstimate(
-            flops=2 * pair.size * channels, bytes_accessed=6 * pair.size, transcendentals=pair.size
-        ),
-        name="gates",
-    )(pair, gain, weight)
 
 
 def update_kernel(
@@ -234,7 +229,7 @@
     width, each = chips * cols, gate_ref.shape[1]
     channels = gate_ref.shape[4]
     odd = odd_ref[0]
-    gain = jnp.broadcast_to(gain_ref[...], (here_k, width)).T.reshape(width, 1, here_k)
+    gain = gain_ref[...].reshape(width, 1, here_k)
     outgoing = []
     for c in range(cores):
         product = back_ref[:, c].reshape(width, half, here_k).astype(F32)
@@ -297,15 +292,14 @@
     got = got.reshape(rows, cols, 2, half, here_k)
     right = split(got)
     other = lax.ppermute(right, "row", [(r, r ^ 1) for r in range(rows)])
-    left, own = own_part(got, right)
+    left, own, gate, columns, halved = own_part(
+        got, right, pair, gain, gate_weight, ln_out_gain.reshape(1, width), out_weight
+    )
     product = merge(left, own, other, (rows, cols, half, here_k))
-    product, late_pair = lax.optimization_barrier((product, pair))
+    odd = lax.rem(lax.axis_index("col"), 2).reshape(1)
+    product, odd = lax.optimization_barrier((product, odd))
     back = exchange(product.reshape(rows * cols, half, here_k))
-    gate = gates(late_pair, gain, gate_weight)
-    odd = lax.rem(lax.axis_index("col"), 2).reshape(1)
-    return updates(
-        odd, back.reshape(chips, 2, cols, half, here_k), ln_out_gain.reshape(1, width), out_weight, gate
-    )
+    return updates(odd, back.reshape(chips, 2, cols, half, here_k), columns, halved, gate)
 
 
 def solution(mesh):

time: 116 us -> 117 us (level)
  blocking collectives: 68.6 us -> 105 us
  waiting for transfers between devices: 29 us -> 0.01 us
  starting transfers between devices: 6.74 us -> 0.09 us
  local copies, waits for them, and re-layouts: 1.24 us -> 0 us
    all_to_all x0 -> x1, blocking collectives: none -> 36.9 us  [shards(): back = exchange(product.reshape(rows * cols, half, here_k))]
    all_to_all x1 -> x0, waiting for transfers between devices: 27.1 us -> none  [shards(): back = exchange(product.reshape(rows * cols, half, here_k))]
    all_to_all x1 -> x0, starting transfers between devices: 6.65 us -> none  [shards(): back = exchange(product.reshape(rows * cols, half, here_k))]
    ppermute x1, waiting for transfers between devices: 1.89 us -> 0.01 us  [shards(): other = lax.ppermute(right, 'row', [(r, r ^ 1) for r in range(rows)])]
    unnamed x10 -> x0, local copies, waits for them, and re-layouts: 1.24 us -> none
    pallas_call x3 -> x2, Pallas kernels: 4.47 us -> 5.13 us  [the longest x1 3.16 us: own_part(): pl.pallas_call(own_kernel, in_specs=[vmem] * 2 + [hbm] * 5, out_specs=[vm...]
  transfers between devices with their start and end apart: 2 -> 1, of which waited for: 2 -> 0; matrix products, arithmetic and copies ran while one was open for 0% -> 0% of each run, Pallas kernels for 2% -> 3%
where the time goes in v11:
time: 117 us
  blocking collectives  105 us (90%)
  Pallas kernels  11.1 us (9%)
    all_to_all x1, blocking collectives, shards(): got = exchange(sent.reshape(rows * cols, 2, half, here_k))  68.6 us
    all_to_all x1, blocking collectives, shards(): back = exchange(product.reshape(rows * cols, half, here_k))  36.9 us
    pallas_call x1, Pallas kernels, operands(): pl.pallas_call(operands_kernel, in_specs=[hbm] * 4, out_specs=pl.BlockSpe...  3.41 us
    pallas_call x1, Pallas kernels, own_part(): pl.pallas_call(own_kernel, in_specs=[vmem] * 2 + [hbm] * 5, out_specs=[vm...  3.16 us
  transfers between devices with their start and end apart: 1, of which 0 were waited for; matrix products, arithmetic and copies ran while one was open for 0% of the time, Pallas kernels for 3%

profile of v11, /device:TPU:1, one launch (start us, length us, event | category | flops | bytes accessed | tf_op | source)
XLA Modules:
  0.0 116.7 jit_solution(17596081982917313628)
XLA Ops:
  0.0 3.4 %operands.1 = bf16[16,2,8,2,16,128]{5,4,3,2,1,0:T(8,128)(2,1)S(1)} custom-call(bf16[32,128,128]{2,1,0:T(8,128)(2,1)} %pair_hbm.3, f32[1,128]{1,0:T(1,128)} %bitcast.15, bf16[128,256]{1,0:T(8,128)(2,1)} %left_hbm.1, bf16[128,256]{1,0:T(8,128)(2,1)} %right_hbm.1), custom_call_target="tpu_custom_call" | custom-call | tf_op jit(solution)/shard_map/operands/pallas_call | solution.py:77
  3.4 68.6 %all_to_all.10 = bf16[256,2,16,128]{3,2,1,0:T(8,128)(2,1)S(1)} all-to-all(bf16[256,2,16,128]{3,2,1,0:T(8,128)(2,1)S(1)} %bitcast.11), channel_id=1, replica_groups=mesh['row'=32,'col'=8] {'row','col'}, dimensions={0} | all-to-all | bytes 4194304 | tf_op jit(solution)/shard_map/all_to_all | solution.py:291
  72.0 0.3 split.1.right_ref
  72.3 0.1 collective-permute-start
  72.4 3.2 %own_part.1 = (bf16[512,1024]{1,0:T(8,128)(2,1)S(1)}, bf16[512,512]{1,0:T(8,128)(2,1)S(1)}, f32[32,128,128]{2,1,0:T(8,128)S(1)}, f32[128,128]{1,0:T(8,128)S(1)}, bf16[128,128]{1,0:T(8,128)(2,1)S(1)}) custom-call(bf16[32,8,2,16,128]{4,3,2,1,0:T(8,128)(2,1)S(1)} %bitcast.10, bf16[512,1024]{1,0:T(8,128)(2,1)S(1)} %split.1.right_ref, ...), custom_call_target="tpu_custom_call" | custom-call | flops 536870912 | bytes 4194304 | tf_op jit(solution)/shard_map/own_part/pallas_call | solution.py:162
  75.6 0.0 collective-permute-done.other_ref
  75.6 2.0 %merge.1 = bf16[32,8,16,128]{3,2,1,0:T(8,128)(2,1)S(1)} custom-call(bf16[512,1024]{1,0:T(8,128)(2,1)S(1)} %get-tuple-element.12.left_ref, bf16[512,512]{1,0:T(8,128)(2,1)S(1)} %get-tuple-element.13.own_ref, bf16[512,1024]{1,0:T(8,128)(2,1)} %collective-permute-done.other_ref), custom_call_target="tpu_custom_call" | custom-call | tf_op jit(solution)/shard_map/merge/pallas_call | solution.py:215
  77.6 36.9 %all_to_all.11 = bf16[256,16,128]{2,1,0:T(8,128)(2,1)S(1)} all-to-all(bf16[256,16,128]{2,1,0:T(8,128)(2,1)S(1)} %bitcast.13), channel_id=1, replica_groups=mesh['row'=32,'col'=8] {'row','col'}, dimensions={0} | all-to-all | bytes 2097152 | tf_op jit(solution)/shard_map/all_to_all | solution.py:301
  114.5 2.3 %updates.1 = bf16[32,4,2,16,128]{4,3,2,1,0:T(8,128)(2,1)} custom-call(s32[1]{0:T(128)} %bitcast.4.odd_ref, bf16[16,2,8,16,128]{4,3,2,1,0:T(8,128)(2,1)S(1)} %bitcast.12, f32[128,128]{1,0:T(8,128)S(1)} %get-tuple-element.16.gain_ref, bf16[128,128]{1,0:T(8,128)(2,1)S(1)} %get-tuple-element.17.weight_ref, f32[32,4,2,16,128]{4,3,2,1,0:T(8,128)S(1)} %bitcast.14), custom_call_target="tpu_custom_call" | custom-call | tf_op jit(solution)/shard_map/updates/pallas_call | solution.py:266
Async XLA Ops:
  72.3 3.3 %collective-permute-start = (bf16[512,1024]{1,0:T(8,128)(2,1)S(1)}, bf16[512,1024]{1,0:T(8,128)(2,1)}, u32[]{:S(2)}, u32[]{:S(2)}) collective-permute-start(bf16[512,1024]{1,0:T(8,128)(2,1)S(1)} %split.1.right_ref), channel_id=1, source_target_pairs={{0,8},{8,0},{16,24},{24,16},{32,40},{40,32},{48,56},{56,48},{64,72... | collective-permute-start | bytes 3145736 | tf_op jit(solution)/shard_map/ppermute | solution.py:294
